TPU v7x, 32 devices: a whole 2x2x4 slice. The times are simulated.
32 devices in a mesh: wide: 8 (over z, x), deep: 4 (over y, core).
Axes of the slice: x: 2, y: 2, z: 4, core: 2. Of those that a mesh axis runs over, the one named last changes fastest.
Arguments:
- density: bfloat16 [2048, 64, 128], P(('wide', 'deep')), may hold values from -0.1796875 to 0.1796875
- basis_in: bfloat16 [2048, 64, 128], P(('wide', 'deep')), may hold values from -0.5 to 0.5
- basis_out: bfloat16 [2048, 64, 128], P(('wide', 'deep')), may hold values from -0.75 to 0.75
- points: bfloat16 [2048, 3, 128], P(('wide', 'deep')), may hold values from 0 to 4
- nodes: bfloat16 [2048, 3, 64], P(('wide', 'deep')), may hold values from 0 to 16
- near_rows: int32 [2048, 27], P(('wide', 'deep')), may hold values from 0 to 2047, as said below
- send_leaf: int32 [32, 32, 8], P(('wide', 'deep')), may hold values from 0 to 63
- adm_slot: int32 [2048, 96], P(('wide', 'deep')), may hold values from 0 to 255
Outputs:
- potential: float32 [2048, 64, 128], P(('wide', 'deep'))
Inputs may be any that keep to these rules, and one draw needn't show every extreme that they name: near_rows[j, 0] = j. Every other entry names a leaf of the device of leaf j, of the next device along deep, or of the next device along wide; leaf j lies on device j // 64, numbered wide index * 4 + deep index.
All inputs are finite; a program needn't handle non-finite values.
Results may differ from a plain program's by a relative error of at most 0.0033.
Values may be sent and summed in bfloat16 or wider, within the bound.
A program may use at most 128 MiB of HBM per device.

v0:
```python
import jax
import jax.numpy as jnp
from jax import lax
from jax.sharding import PartitionSpec as P

SOFTENING = 0.25


def passed_along(x, axis, by):
    length = lax.axis_size(axis)
    pairs = [(i, i + by) for i in range(length) if 0 <= i + by < length]
    return lax.ppermute(x, axis, pairs)


def pair_kernel(targets, sources):
    differ = targets[..., 0, :, None] - sources[..., 0, None, :]
    squared = differ * differ
    for coord in range(1, 3):
        differ = targets[..., coord, :, None] - sources[..., coord, None, :]
        squared = squared + differ * differ
    return 1.0 / jnp.sqrt(squared + SOFTENING)


def pick_rows(indices, table):
    width = table.shape[0]
    selector = (indices.reshape(-1)[:, None] == jnp.arange(width, dtype=jnp.int32)[None, :]).astype(
        jnp.bfloat16
    )
    picked = jnp.dot(selector, table.reshape(width, -1), preferred_element_type=jnp.float32)
    return picked.reshape(indices.shape + table.shape[1:])


def add_rows(totals, selector, partial_flat):
    return totals + lax.dot_general(
        selector,
        partial_flat,
        (((0,), (0,)), ((), ())),
        precision=lax.Precision.HIGHEST,
        preferred_element_type=jnp.float32,
    )


def shards(density, basis_in, basis_out, points, nodes, near_rows, send_leaf, adm_slot):
    leaves = density.shape[0]
    fields = density.shape[1]
    leaf_size = density.shape[2]
    rank_size = basis_in.shape[1]
    adm_count = adm_slot.shape[1]
    near_count = near_rows.shape[1]
    wide_count = lax.axis_size("wide")
    deep_count = lax.axis_size("deep")
    devices = wide_count * deep_count
    capacity = send_leaf.shape[2]
    turns = 8
    block_size = leaves // turns
    coefficients = jnp.einsum(
        "jrp,jnp->jrn", basis_in, density, preferred_element_type=jnp.float32
    ).astype(jnp.bfloat16)
    send_local = send_leaf.reshape(devices, capacity)
    outgoing = coefficients[send_local].reshape(devices, capacity, rank_size * fields)
    out_nodes = nodes[send_local].reshape(devices, capacity, 3 * rank_size)
    table, table_nodes = (
        lax.all_to_all(outgoing, ("wide", "deep"), split_axis=0, concat_axis=0, tiled=True),
        lax.all_to_all(out_nodes, ("wide", "deep"), split_axis=0, concat_axis=0, tiled=True),
    )
    table = table.reshape(devices * capacity, rank_size, fields)
    table_nodes = table_nodes.reshape(devices * capacity, 3 * rank_size)

    def far_block(items):
        slots, row_nodes, out_basis = items
        gathered = table[slots]
        far_nodes = pick_rows(slots, table_nodes).reshape(block_size, adm_count, 3, rank_size)
        coupling = pair_kernel(row_nodes[:, None].astype(jnp.float32), far_nodes).astype(
            jnp.bfloat16
        )
        far_coef = jnp.einsum(
            "iarb,iabn->irn", coupling, gathered, preferred_element_type=jnp.float32
        ).astype(jnp.bfloat16)
        return jnp.einsum("irn,irp->inp", far_coef, out_basis, preferred_element_type=jnp.float32)

    far_field = lax.map(
        far_block,
        (
            adm_slot.reshape(turns, block_size, adm_count),
            nodes.reshape(turns, block_size, 3, rank_size),
            basis_out.reshape(turns, block_size, rank_size, leaf_size),
        ),
    )
    far_field = far_field.reshape(leaves, fields, leaf_size)
    my_device = lax.axis_index("wide") * deep_count + lax.axis_index("deep")
    deep_points = passed_along(points, "deep", -1)
    wide_points = passed_along(points, "wide", -1)
    point_table = jnp.concatenate([points, deep_points, wide_points], axis=0)
    offset = near_rows // leaves - my_device
    region = jnp.where(offset == 0, 0, jnp.where(offset == 1, 1, 2))
    codes = region * leaves + near_rows % leaves
    row_range = jnp.arange(3 * leaves, dtype=jnp.int32)

    def near_step(totals, items):
        dens_block, own_points, targets = items
        target_points = pick_rows(targets, point_table)
        kernel_block = pair_kernel(target_points, own_points[:, None].astype(jnp.float32)).astype(
            jnp.bfloat16
        )
        partial_sums = jnp.einsum(
            "jkab,jnb->jkna", kernel_block, dens_block, preferred_element_type=jnp.float32
        )
        selector = (targets.reshape(-1)[:, None] == row_range[None, :]).astype(jnp.float32)
        totals = add_rows(totals, selector, partial_sums.reshape(-1, fields * leaf_size))
        return (totals, None)

    start_totals = jnp.zeros((3 * leaves, fields * leaf_size), jnp.float32)
    totals, _ = lax.scan(
        near_step,
        start_totals,
        (
            density.reshape(turns, block_size, fields, leaf_size),
            points.reshape(turns, block_size, 3, leaf_size),
            codes.reshape(turns, block_size, near_count),
        ),
    )
    totals = totals.reshape(3, leaves, fields, leaf_size)
    from_deep = passed_along(totals[1], "deep", 1)
    from_wide = passed_along(totals[2], "wide", 1)
    near_field = totals[0] + from_deep + from_wide
    return far_field + near_field


def solution(mesh):
    in_specs = (
        P(("wide", "deep"), None, None),
        P(("wide", "deep"), None, None),
        P(("wide", "deep"), None, None),
        P(("wide", "deep"), None, None),
        P(("wide", "deep"), None, None),
        P(("wide", "deep"), None),
        P(("wide", "deep"), None, None),
        P(("wide", "deep"), None),
    )
    out_specs = P(("wide", "deep"), None, None)
    return jax.shard_map(shards, mesh=mesh, in_specs=in_specs, out_specs=out_specs, check_vma=False)
```

profile of v0, /device:TPU:0, one launch (start us, length us, event | category | flops | bytes accessed | tf_op | source)
XLA Modules:
  0.0 846.3 jit_solution(7219741778683485754)
XLA Ops:
  16.0 9.4 %all-to-all-start.1 = ((bf16[32,8,4096]{2,1,0:T(8,128)(2,1)}), bf16[32,8,4096]{2,1,0:T(8,128)(2,1)S(1)}, u32[]{:S(2)}, u32[]{:S(2)}) async-start(bf16[32,8,4096]{2,1,0:T(8,128)(2,1)} %reshape.182), calls=%async_computation.1 | async-start | bytes 4194304 | tf_op jit(solution)/shard_map/all_to_all | solution.py:63
  28.1 271.0 %while.22 = (s32[]{:T(128)}, f32[192,8192]{1,0:T(8,128)}, s32[8,8,27]{2,1,0:T(8,128)S(1)}, bf16[8,8,64,128]{3,2,1,0:T(8,128)(2,1)}, bf16[192,3,128]{2,1,0:T(4,12...) while((s32[]{:T(128)}, f32[192,8192]{1,0:T(8,128)}, ...), condition=%wide.region_3.4_spmd.clone, body=%wide.region_2.3_spmd.clone.sunk | while | flops 4600320000 | bytes 72446912 | solution.py:113
  29.3 20.3 %fusion.63 = f32[8,64,27,128]{3,1,2,0:T(8,128)S(1)} fusion(f32[8,128]{1,0:T(8,128)S(1)} %get-tuple-element.274, f32[8,27,128]{2,1,0:T(8,128)S(1)} %get-tuple-element.275, f32[8,128]{1,0:T(8,128)S(1)} %get-tuple-element.276, f32[8,27,128]{2,1,0:T(8,128)S(1)} %get-tuple-element.277, f32[8,128]{1,0:T(8,128)S(1)} %get-tuple-element.278, ...), kind=kOutput, calls=%fused_computation.27.clone.1 | convolution fusion | flops 488374272 | bytes 7553028 | tf_op jit(solution)/shard_map/while/body/eval_jaxpr/jkab,jnb->jkna/dot_general | solution.py:105
  49.6 9.7 %convolution_add_fusion.2 = f32[192,8192]{1,0:T(8,128)S(1)} fusion(f32[27,8,64,128]{3,2,1,0:T(8,128)S(1)} %bitcast.174, f32[192,8192]{1,0:T(8,128)S(1)} %bitcast.173, pred[]{:T(512)S(6)} %compare.6, s32[216]{0:T(256)S(1)} %eq.129), kind=kOutput, calls=%fused_computation.26.clone.1 | convolution fusion | flops 4080050688 | bytes 19661664 | tf_op jit(solution)/shard_map/while/body/eval_jaxpr/dot_general | solution.py:34
  63.2 20.3 %fusion.63 = f32[8,64,27,128]{3,1,2,0:T(8,128)S(1)} fusion(f32[8,128]{1,0:T(8,128)S(1)} %get-tuple-element.274, f32[8,27,128]{2,1,0:T(8,128)S(1)} %get-tuple-element.275, f32[8,128]{1,0:T(8,128)S(1)} %get-tuple-element.276, f32[8,27,128]{2,1,0:T(8,128)S(1)} %get-tuple-element.277, f32[8,128]{1,0:T(8,128)S(1)} %get-tuple-element.278, ...), kind=kOutput, calls=%fused_computation.27.clone.1 | convolution fusion | flops 488374272 | bytes 7553028 | tf_op jit(solution)/shard_map/while/body/eval_jaxpr/jkab,jnb->jkna/dot_general | solution.py:105
  83.5 9.7 %convolution_add_fusion.2 = f32[192,8192]{1,0:T(8,128)S(1)} fusion(f32[27,8,64,128]{3,2,1,0:T(8,128)S(1)} %bitcast.174, f32[192,8192]{1,0:T(8,128)S(1)} %bitcast.173, pred[]{:T(512)S(6)} %compare.6, s32[216]{0:T(256)S(1)} %eq.129), kind=kOutput, calls=%fused_computation.26.clone.1 | convolution fusion | flops 4080050688 | bytes 19661664 | tf_op jit(solution)/shard_map/while/body/eval_jaxpr/dot_general | solution.py:34
  97.0 20.3 %fusion.63 = f32[8,64,27,128]{3,1,2,0:T(8,128)S(1)} fusion(f32[8,128]{1,0:T(8,128)S(1)} %get-tuple-element.274, f32[8,27,128]{2,1,0:T(8,128)S(1)} %get-tuple-element.275, f32[8,128]{1,0:T(8,128)S(1)} %get-tuple-element.276, f32[8,27,128]{2,1,0:T(8,128)S(1)} %get-tuple-element.277, f32[8,128]{1,0:T(8,128)S(1)} %get-tuple-element.278, ...), kind=kOutput, calls=%fused_computation.27.clone.1 | convolution fusion | flops 488374272 | bytes 7553028 | tf_op jit(solution)/shard_map/while/body/eval_jaxpr/jkab,jnb->jkna/dot_general | solution.py:105
  117.4 9.7 %convolution_add_fusion.2 = f32[192,8192]{1,0:T(8,128)S(1)} fusion(f32[27,8,64,128]{3,2,1,0:T(8,128)S(1)} %bitcast.174, f32[192,8192]{1,0:T(8,128)S(1)} %bitcast.173, pred[]{:T(512)S(6)} %compare.6, s32[216]{0:T(256)S(1)} %eq.129), kind=kOutput, calls=%fused_computation.26.clone.1 | convolution fusion | flops 4080050688 | bytes 19661664 | tf_op jit(solution)/shard_map/while/body/eval_jaxpr/dot_general | solution.py:34
  130.9 20.3 %fusion.63 = f32[8,64,27,128]{3,1,2,0:T(8,128)S(1)} fusion(f32[8,128]{1,0:T(8,128)S(1)} %get-tuple-element.274, f32[8,27,128]{2,1,0:T(8,128)S(1)} %get-tuple-element.275, f32[8,128]{1,0:T(8,128)S(1)} %get-tuple-element.276, f32[8,27,128]{2,1,0:T(8,128)S(1)} %get-tuple-element.277, f32[8,128]{1,0:T(8,128)S(1)} %get-tuple-element.278, ...), kind=kOutput, calls=%fused_computation.27.clone.1 | convolution fusion | flops 488374272 | bytes 7553028 | tf_op jit(solution)/shard_map/while/body/eval_jaxpr/jkab,jnb->jkna/dot_general | solution.py:105
  151.3 9.7 %convolution_add_fusion.2 = f32[192,8192]{1,0:T(8,128)S(1)} fusion(f32[27,8,64,128]{3,2,1,0:T(8,128)S(1)} %bitcast.174, f32[192,8192]{1,0:T(8,128)S(1)} %bitcast.173, pred[]{:T(512)S(6)} %compare.6, s32[216]{0:T(256)S(1)} %eq.129), kind=kOutput, calls=%fused_computation.26.clone.1 | convolution fusion | flops 4080050688 | bytes 19661664 | tf_op jit(solution)/shard_map/while/body/eval_jaxpr/dot_general | solution.py:34
  164.8 20.3 %fusion.63 = f32[8,64,27,128]{3,1,2,0:T(8,128)S(1)} fusion(f32[8,128]{1,0:T(8,128)S(1)} %get-tuple-element.274, f32[8,27,128]{2,1,0:T(8,128)S(1)} %get-tuple-element.275, f32[8,128]{1,0:T(8,128)S(1)} %get-tuple-element.276, f32[8,27,128]{2,1,0:T(8,128)S(1)} %get-tuple-element.277, f32[8,128]{1,0:T(8,128)S(1)} %get-tuple-element.278, ...), kind=kOutput, calls=%fused_computation.27.clone.1 | convolution fusion | flops 488374272 | bytes 7553028 | tf_op jit(solution)/shard_map/while/body/eval_jaxpr/jkab,jnb->jkna/dot_general | solution.py:105
  185.1 9.7 %convolution_add_fusion.2 = f32[192,8192]{1,0:T(8,128)S(1)} fusion(f32[27,8,64,128]{3,2,1,0:T(8,128)S(1)} %bitcast.174, f32[192,8192]{1,0:T(8,128)S(1)} %bitcast.173, pred[]{:T(512)S(6)} %compare.6, s32[216]{0:T(256)S(1)} %eq.129), kind=kOutput, calls=%fused_computation.26.clone.1 | convolution fusion | flops 4080050688 | bytes 19661664 | tf_op jit(solution)/shard_map/while/body/eval_jaxpr/dot_general | solution.py:34
  198.6 20.3 %fusion.63 = f32[8,64,27,128]{3,1,2,0:T(8,128)S(1)} fusion(f32[8,128]{1,0:T(8,128)S(1)} %get-tuple-element.274, f32[8,27,128]{2,1,0:T(8,128)S(1)} %get-tuple-element.275, f32[8,128]{1,0:T(8,128)S(1)} %get-tuple-element.276, f32[8,27,128]{2,1,0:T(8,128)S(1)} %get-tuple-element.277, f32[8,128]{1,0:T(8,128)S(1)} %get-tuple-element.278, ...), kind=kOutput, calls=%fused_computation.27.clone.1 | convolution fusion | flops 488374272 | bytes 7553028 | tf_op jit(solution)/shard_map/while/body/eval_jaxpr/jkab,jnb->jkna/dot_general | solution.py:105
  219.0 9.7 %convolution_add_fusion.2 = f32[192,8192]{1,0:T(8,128)S(1)} fusion(f32[27,8,64,128]{3,2,1,0:T(8,128)S(1)} %bitcast.174, f32[192,8192]{1,0:T(8,128)S(1)} %bitcast.173, pred[]{:T(512)S(6)} %compare.6, s32[216]{0:T(256)S(1)} %eq.129), kind=kOutput, calls=%fused_computation.26.clone.1 | convolution fusion | flops 4080050688 | bytes 19661664 | tf_op jit(solution)/shard_map/while/body/eval_jaxpr/dot_general | solution.py:34
  232.5 20.3 %fusion.63 = f32[8,64,27,128]{3,1,2,0:T(8,128)S(1)} fusion(f32[8,128]{1,0:T(8,128)S(1)} %get-tuple-element.274, f32[8,27,128]{2,1,0:T(8,128)S(1)} %get-tuple-element.275, f32[8,128]{1,0:T(8,128)S(1)} %get-tuple-element.276, f32[8,27,128]{2,1,0:T(8,128)S(1)} %get-tuple-element.277, f32[8,128]{1,0:T(8,128)S(1)} %get-tuple-element.278, ...), kind=kOutput, calls=%fused_computation.27.clone.1 | convolution fusion | flops 488374272 | bytes 7553028 | tf_op jit(solution)/shard_map/while/body/eval_jaxpr/jkab,jnb->jkna/dot_general | solution.py:105
  252.9 9.7 %convolution_add_fusion.2 = f32[192,8192]{1,0:T(8,128)S(1)} fusion(f32[27,8,64,128]{3,2,1,0:T(8,128)S(1)} %bitcast.174, f32[192,8192]{1,0:T(8,128)S(1)} %bitcast.173, pred[]{:T(512)S(6)} %compare.6, s32[216]{0:T(256)S(1)} %eq.129), kind=kOutput, calls=%fused_computation.26.clone.1 | convolution fusion | flops 4080050688 | bytes 19661664 | tf_op jit(solution)/shard_map/while/body/eval_jaxpr/dot_general | solution.py:34
  266.3 20.3 %fusion.63 = f32[8,64,27,128]{3,1,2,0:T(8,128)S(1)} fusion(f32[8,128]{1,0:T(8,128)S(1)} %get-tuple-element.274, f32[8,27,128]{2,1,0:T(8,128)S(1)} %get-tuple-element.275, f32[8,128]{1,0:T(8,128)S(1)} %get-tuple-element.276, f32[8,27,128]{2,1,0:T(8,128)S(1)} %get-tuple-element.277, f32[8,128]{1,0:T(8,128)S(1)} %get-tuple-element.278, ...), kind=kOutput, calls=%fused_computation.27.clone.1 | convolution fusion | flops 488374272 | bytes 7553028 | tf_op jit(solution)/shard_map/while/body/eval_jaxpr/jkab,jnb->jkna/dot_general | solution.py:105
  286.7 9.7 %convolution_add_fusion.2 = f32[192,8192]{1,0:T(8,128)S(1)} fusion(f32[27,8,64,128]{3,2,1,0:T(8,128)S(1)} %bitcast.174, f32[192,8192]{1,0:T(8,128)S(1)} %bitcast.173, pred[]{:T(512)S(6)} %compare.6, s32[216]{0:T(256)S(1)} %eq.129), kind=kOutput, calls=%fused_computation.26.clone.1 | convolution fusion | flops 4080050688 | bytes 19661664 | tf_op jit(solution)/shard_map/while/body/eval_jaxpr/dot_general | solution.py:34
  327.0 513.3 %while.21 = (s32[]{:T(128)}, f32[8,8,64,128]{3,2,1,0:T(8,128)}, bf16[8,8,3,64]{3,1,0,2:T(8,128)(2,1)S(1)}, s32[8,8,96]{2,1,0:T(8,128)}, bf16[256,192]{1,0:T(8,12...) while((s32[]{:T(128)}, f32[8,8,64,128]{3,2,1,0:T(8,128)}, ...), condition=%wide.region_1.2_spmd, body=%wide.region_0.1_spmd.sunk | while | flops 518230784 | bytes 61896804 | solution.py:81
  328.9 7.7 rsqrt_convert_fusion.5
  336.6 20.8 %copy.89 = bf16[8,96,64,64]{3,2,1,0:T(8,128)(2,1)} copy(bf16[8,96,64,64]{1,3,2,0:T(8,128)(2,1)} %rsqrt_convert_fusion.5) | data formatting | bytes 12582912 | tf_op jit(solution)/shard_map/while/body/eval_jaxpr/convert_element_type | solution.py:73
  357.5 21.8 %gather_fusion = bf16[768,64,64]{2,1,0:T(8,128)(2,1)} fusion(bf16[256,64,64]{2,1,0:T(8,128)(2,1)} %get-tuple-element.325, s32[1024]{0:T(1024)S(1)} %pad_clamp_fusion.3), kind=kCustom, calls=%fused_computation.clone.1 | custom fusion | bytes 12585984 | tf_op jit(solution)/shard_map/while/body/eval_jaxpr/gather | solution.py:71
  379.3 11.8 %fusion.57 = f32[8,8,64,128]{3,2,1,0:T(8,128)} fusion(f32[8,8,64,128]{3,2,1,0:T(8,128)} %get-tuple-element.313, s32[]{:T(128)S(6)} %copy.102, bf16[8,96,64,64]{3,2,1,0:T(8,128)(2,1)} %copy.89, bf16[8,96,64,64]{3,2,1,0:T(8,128)(2,1)} %bitcast.171, bf16[8,8,64,128]{3,2,1,0:T(8,128)(2,1)} %get-tuple-element.326), kind=kOutput, calls=%fused_computation.6.clone.1 | convolution fusion | flops 411074560 | bytes 25560064 | tf_op jit(solution)/shard_map/while/body/eval_jaxpr/irn,irp->inp/dot_general | solution.py:79
  393.1 7.7 rsqrt_convert_fusion.5
  400.8 20.8 %copy.89 = bf16[8,96,64,64]{3,2,1,0:T(8,128)(2,1)} copy(bf16[8,96,64,64]{1,3,2,0:T(8,128)(2,1)} %rsqrt_convert_fusion.5) | data formatting | bytes 12582912 | tf_op jit(solution)/shard_map/while/body/eval_jaxpr/convert_element_type | solution.py:73
  421.6 21.8 %gather_fusion = bf16[768,64,64]{2,1,0:T(8,128)(2,1)} fusion(bf16[256,64,64]{2,1,0:T(8,128)(2,1)} %get-tuple-element.325, s32[1024]{0:T(1024)S(1)} %pad_clamp_fusion.3), kind=kCustom, calls=%fused_computation.clone.1 | custom fusion | bytes 12585984 | tf_op jit(solution)/shard_map/while/body/eval_jaxpr/gather | solution.py:71
  443.5 11.8 %fusion.57 = f32[8,8,64,128]{3,2,1,0:T(8,128)} fusion(f32[8,8,64,128]{3,2,1,0:T(8,128)} %get-tuple-element.313, s32[]{:T(128)S(6)} %copy.102, bf16[8,96,64,64]{3,2,1,0:T(8,128)(2,1)} %copy.89, bf16[8,96,64,64]{3,2,1,0:T(8,128)(2,1)} %bitcast.171, bf16[8,8,64,128]{3,2,1,0:T(8,128)(2,1)} %get-tuple-element.326), kind=kOutput, calls=%fused_computation.6.clone.1 | convolution fusion | flops 411074560 | bytes 25560064 | tf_op jit(solution)/shard_map/while/body/eval_jaxpr/irn,irp->inp/dot_general | solution.py:79
  457.2 7.7 rsqrt_convert_fusion.5
  464.9 20.8 %copy.89 = bf16[8,96,64,64]{3,2,1,0:T(8,128)(2,1)} copy(bf16[8,96,64,64]{1,3,2,0:T(8,128)(2,1)} %rsqrt_convert_fusion.5) | data formatting | bytes 12582912 | tf_op jit(solution)/shard_map/while/body/eval_jaxpr/convert_element_type | solution.py:73
  485.8 21.8 %gather_fusion = bf16[768,64,64]{2,1,0:T(8,128)(2,1)} fusion(bf16[256,64,64]{2,1,0:T(8,128)(2,1)} %get-tuple-element.325, s32[1024]{0:T(1024)S(1)} %pad_clamp_fusion.3), kind=kCustom, calls=%fused_computation.clone.1 | custom fusion | bytes 12585984 | tf_op jit(solution)/shard_map/while/body/eval_jaxpr/gather | solution.py:71
  507.6 11.8 %fusion.57 = f32[8,8,64,128]{3,2,1,0:T(8,128)} fusion(f32[8,8,64,128]{3,2,1,0:T(8,128)} %get-tuple-element.313, s32[]{:T(128)S(6)} %copy.102, bf16[8,96,64,64]{3,2,1,0:T(8,128)(2,1)} %copy.89, bf16[8,96,64,64]{3,2,1,0:T(8,128)(2,1)} %bitcast.171, bf16[8,8,64,128]{3,2,1,0:T(8,128)(2,1)} %get-tuple-element.326), kind=kOutput, calls=%fused_computation.6.clone.1 | convolution fusion | flops 411074560 | bytes 25560064 | tf_op jit(solution)/shard_map/while/body/eval_jaxpr/irn,irp->inp/dot_general | solution.py:79
  521.3 7.7 rsqrt_convert_fusion.5
  529.1 20.8 %copy.89 = bf16[8,96,64,64]{3,2,1,0:T(8,128)(2,1)} copy(bf16[8,96,64,64]{1,3,2,0:T(8,128)(2,1)} %rsqrt_convert_fusion.5) | data formatting | bytes 12582912 | tf_op jit(solution)/shard_map/while/body/eval_jaxpr/convert_element_type | solution.py:73
  549.9 21.8 %gather_fusion = bf16[768,64,64]{2,1,0:T(8,128)(2,1)} fusion(bf16[256,64,64]{2,1,0:T(8,128)(2,1)} %get-tuple-element.325, s32[1024]{0:T(1024)S(1)} %pad_clamp_fusion.3), kind=kCustom, calls=%fused_computation.clone.1 | custom fusion | bytes 12585984 | tf_op jit(solution)/shard_map/while/body/eval_jaxpr/gather | solution.py:71
  571.8 11.8 %fusion.57 = f32[8,8,64,128]{3,2,1,0:T(8,128)} fusion(f32[8,8,64,128]{3,2,1,0:T(8,128)} %get-tuple-element.313, s32[]{:T(128)S(6)} %copy.102, bf16[8,96,64,64]{3,2,1,0:T(8,128)(2,1)} %copy.89, bf16[8,96,64,64]{3,2,1,0:T(8,128)(2,1)} %bitcast.171, bf16[8,8,64,128]{3,2,1,0:T(8,128)(2,1)} %get-tuple-element.326), kind=kOutput, calls=%fused_computation.6.clone.1 | convolution fusion | flops 411074560 | bytes 25560064 | tf_op jit(solution)/shard_map/while/body/eval_jaxpr/irn,irp->inp/dot_general | solution.py:79
  585.5 7.7 rsqrt_convert_fusion.5
  593.3 20.8 %copy.89 = bf16[8,96,64,64]{3,2,1,0:T(8,128)(2,1)} copy(bf16[8,96,64,64]{1,3,2,0:T(8,128)(2,1)} %rsqrt_convert_fusion.5) | data formatting | bytes 12582912 | tf_op jit(solution)/shard_map/while/body/eval_jaxpr/convert_element_type | solution.py:73
  614.1 21.8 %gather_fusion = bf16[768,64,64]{2,1,0:T(8,128)(2,1)} fusion(bf16[256,64,64]{2,1,0:T(8,128)(2,1)} %get-tuple-element.325, s32[1024]{0:T(1024)S(1)} %pad_clamp_fusion.3), kind=kCustom, calls=%fused_computation.clone.1 | custom fusion | bytes 12585984 | tf_op jit(solution)/shard_map/while/body/eval_jaxpr/gather | solution.py:71
  635.9 11.8 %fusion.57 = f32[8,8,64,128]{3,2,1,0:T(8,128)} fusion(f32[8,8,64,128]{3,2,1,0:T(8,128)} %get-tuple-element.313, s32[]{:T(128)S(6)} %copy.102, bf16[8,96,64,64]{3,2,1,0:T(8,128)(2,1)} %copy.89, bf16[8,96,64,64]{3,2,1,0:T(8,128)(2,1)} %bitcast.171, bf16[8,8,64,128]{3,2,1,0:T(8,128)(2,1)} %get-tuple-element.326), kind=kOutput, calls=%fused_computation.6.clone.1 | convolution fusion | flops 411074560 | bytes 25560064 | tf_op jit(solution)/shard_map/while/body/eval_jaxpr/irn,irp->inp/dot_general | solution.py:79
  657.4 20.8 %copy.89 = bf16[8,96,64,64]{3,2,1,0:T(8,128)(2,1)} copy(bf16[8,96,64,64]{1,3,2,0:T(8,128)(2,1)} %rsqrt_convert_fusion.5) | data formatting | bytes 12582912 | tf_op jit(solution)/shard_map/while/body/eval_jaxpr/convert_element_type | solution.py:73
  678.2 21.8 %gather_fusion = bf16[768,64,64]{2,1,0:T(8,128)(2,1)} fusion(bf16[256,64,64]{2,1,0:T(8,128)(2,1)} %get-tuple-element.325, s32[1024]{0:T(1024)S(1)} %pad_clamp_fusion.3), kind=kCustom, calls=%fused_computation.clone.1 | custom fusion | bytes 12585984 | tf_op jit(solution)/shard_map/while/body/eval_jaxpr/gather | solution.py:71
  700.1 11.8 %fusion.57 = f32[8,8,64,128]{3,2,1,0:T(8,128)} fusion(f32[8,8,64,128]{3,2,1,0:T(8,128)} %get-tuple-element.313, s32[]{:T(128)S(6)} %copy.102, bf16[8,96,64,64]{3,2,1,0:T(8,128)(2,1)} %copy.89, bf16[8,96,64,64]{3,2,1,0:T(8,128)(2,1)} %bitcast.171, bf16[8,8,64,128]{3,2,1,0:T(8,128)(2,1)} %get-tuple-element.326), kind=kOutput, calls=%fused_computation.6.clone.1 | convolution fusion | flops 411074560 | bytes 25560064 | tf_op jit(solution)/shard_map/while/body/eval_jaxpr/irn,irp->inp/dot_general | solution.py:79
  721.6 20.8 %copy.89 = bf16[8,96,64,64]{3,2,1,0:T(8,128)(2,1)} copy(bf16[8,96,64,64]{1,3,2,0:T(8,128)(2,1)} %rsqrt_convert_fusion.5) | data formatting | bytes 12582912 | tf_op jit(solution)/shard_map/while/body/eval_jaxpr/convert_element_type | solution.py:73
  742.4 21.8 %gather_fusion = bf16[768,64,64]{2,1,0:T(8,128)(2,1)} fusion(bf16[256,64,64]{2,1,0:T(8,128)(2,1)} %get-tuple-element.325, s32[1024]{0:T(1024)S(1)} %pad_clamp_fusion.3), kind=kCustom, calls=%fused_computation.clone.1 | custom fusion | bytes 12585984 | tf_op jit(solution)/shard_map/while/body/eval_jaxpr/gather | solution.py:71
  764.2 11.9 %fusion.57 = f32[8,8,64,128]{3,2,1,0:T(8,128)} fusion(f32[8,8,64,128]{3,2,1,0:T(8,128)} %get-tuple-element.313, s32[]{:T(128)S(6)} %copy.102, bf16[8,96,64,64]{3,2,1,0:T(8,128)(2,1)} %copy.89, bf16[8,96,64,64]{3,2,1,0:T(8,128)(2,1)} %bitcast.171, bf16[8,8,64,128]{3,2,1,0:T(8,128)(2,1)} %get-tuple-element.326), kind=kOutput, calls=%fused_computation.6.clone.1 | convolution fusion | flops 411074560 | bytes 25560064 | tf_op jit(solution)/shard_map/while/body/eval_jaxpr/irn,irp->inp/dot_general | solution.py:79
  785.7 20.8 %copy.89 = bf16[8,96,64,64]{3,2,1,0:T(8,128)(2,1)} copy(bf16[8,96,64,64]{1,3,2,0:T(8,128)(2,1)} %rsqrt_convert_fusion.5) | data formatting | bytes 12582912 | tf_op jit(solution)/shard_map/while/body/eval_jaxpr/convert_element_type | solution.py:73
  806.6 21.8 %gather_fusion = bf16[768,64,64]{2,1,0:T(8,128)(2,1)} fusion(bf16[256,64,64]{2,1,0:T(8,128)(2,1)} %get-tuple-element.325, s32[1024]{0:T(1024)S(1)} %pad_clamp_fusion.3), kind=kCustom, calls=%fused_computation.clone.1 | custom fusion | bytes 12585984 | tf_op jit(solution)/shard_map/while/body/eval_jaxpr/gather | solution.py:71
  828.4 11.8 %fusion.57 = f32[8,8,64,128]{3,2,1,0:T(8,128)} fusion(f32[8,8,64,128]{3,2,1,0:T(8,128)} %get-tuple-element.313, s32[]{:T(128)S(6)} %copy.102, bf16[8,96,64,64]{3,2,1,0:T(8,128)(2,1)} %copy.89, bf16[8,96,64,64]{3,2,1,0:T(8,128)(2,1)} %bitcast.171, bf16[8,8,64,128]{3,2,1,0:T(8,128)(2,1)} %get-tuple-element.326), kind=kOutput, calls=%fused_computation.6.clone.1 | convolution fusion | flops 411074560 | bytes 25560064 | tf_op jit(solution)/shard_map/while/body/eval_jaxpr/irn,irp->inp/dot_general | solution.py:79
  (252 shorter events, 120.6 us)
Async XLA Ops:
  0.0 4.4 copy-start
  0.9 27.0 %collective-permute-start.1 = (bf16[64,3,128]{2,1,0:T(4,128)(2,1)S(1)}, bf16[64,3,128]{2,1,0:T(4,128)(2,1)S(1)}, u32[]{:S(2)}, u32[]{:S(2)}) collective-permute-start(bf16[64,3,128]{2,1,0:T(4,128)(2,1)S(1)} %copy.54), channel_id=1, source_target_pairs={{4,0},{8,4},{12,8},{16,12},{20,16},{24,20},{28,24},{5,1},{9,5},{13... | collective-permute-start | bytes 147464 | tf_op jit(solution)/shard_map/ppermute | solution.py:12
  2.2 25.7 %collective-permute-start = (bf16[64,3,128]{2,1,0:T(4,128)(2,1)S(1)}, bf16[64,3,128]{2,1,0:T(4,128)(2,1)S(1)}, u32[]{:S(2)}, u32[]{:S(2)}) collective-permute-start(bf16[64,3,128]{2,1,0:T(4,128)(2,1)S(1)} %copy.54), channel_id=1, source_target_pairs={{1,0},{2,1},{3,2},{5,4},{6,5},{7,6},{9,8},{10,9},{11,10},{13,12},{... | collective-permute-start | bytes 147464 | tf_op jit(solution)/shard_map/ppermute | solution.py:12
  9.4 16.0 %copy-start.4 = (s32[64,27]{0,1:T(8,128)S(1)}, s32[64,27]{0,1:T(8,128)}, u32[]{:S(2)}) copy-start(s32[64,27]{0,1:T(8,128)} %param.17) | copy-start | bytes 20740
  9.4 16.2 %copy-start.3 = (bf16[64,3,64]{2,0,1:T(8,128)(2,1)S(1)}, bf16[64,3,64]{2,0,1:T(8,128)(2,1)}, u32[]{:S(2)}) copy-start(bf16[64,3,64]{2,0,1:T(8,128)(2,1)} %param.16) | copy-start | bytes 73732
  16.0 283.1 %all-to-all-start.1 = ((bf16[32,8,4096]{2,1,0:T(8,128)(2,1)}), bf16[32,8,4096]{2,1,0:T(8,128)(2,1)S(1)}, u32[]{:S(2)}, u32[]{:S(2)}) async-start(bf16[32,8,4096]{2,1,0:T(8,128)(2,1)} %reshape.182), calls=%async_computation.1 | async-start | bytes 4194304 | tf_op jit(solution)/shard_map/all_to_all | solution.py:63
  29.2 20.4 %slice-start = ((s8[6291456]{0:T(1024)(128)(4,1)}), s8[4194304]{0:T(1024)(128)(4,1)S(1)}, s32[]{:S(2)}) async-start(s8[6291456]{0:T(1024)(128)(4,1)} %bitcast.172), calls=%async_computation.2 | async-start | bytes 8388608 | tf_op jit(solution)/shard_map/while
  29.3 20.4 %slice-start.1 = ((s8[6291456]{0:T(1024)(128)(4,1)}), s8[2097152]{0:T(1024)(128)(4,1)S(1)}, s32[]{:S(2)}) async-start(s8[6291456]{0:T(1024)(128)(4,1)} %bitcast.172), calls=%async_computation.3 | async-start | bytes 4194304 | tf_op jit(solution)/shard_map/while
  59.3 2.7 copy-start.2
  63.1 20.4 %slice-start = ((s8[6291456]{0:T(1024)(128)(4,1)}), s8[4194304]{0:T(1024)(128)(4,1)S(1)}, s32[]{:S(2)}) async-start(s8[6291456]{0:T(1024)(128)(4,1)} %bitcast.172), calls=%async_computation.2 | async-start | bytes 8388608 | tf_op jit(solution)/shard_map/while
  63.1 20.4 %slice-start.1 = ((s8[6291456]{0:T(1024)(128)(4,1)}), s8[2097152]{0:T(1024)(128)(4,1)S(1)}, s32[]{:S(2)}) async-start(s8[6291456]{0:T(1024)(128)(4,1)} %bitcast.172), calls=%async_computation.3 | async-start | bytes 4194304 | tf_op jit(solution)/shard_map/while
  93.2 2.7 copy-start.2
  97.0 20.4 %slice-start = ((s8[6291456]{0:T(1024)(128)(4,1)}), s8[4194304]{0:T(1024)(128)(4,1)S(1)}, s32[]{:S(2)}) async-start(s8[6291456]{0:T(1024)(128)(4,1)} %bitcast.172), calls=%async_computation.2 | async-start | bytes 8388608 | tf_op jit(solution)/shard_map/while
  97.0 20.4 %slice-start.1 = ((s8[6291456]{0:T(1024)(128)(4,1)}), s8[2097152]{0:T(1024)(128)(4,1)S(1)}, s32[]{:S(2)}) async-start(s8[6291456]{0:T(1024)(128)(4,1)} %bitcast.172), calls=%async_computation.3 | async-start | bytes 4194304 | tf_op jit(solution)/shard_map/while
  127.1 2.7 copy-start.2
  130.8 20.4 %slice-start = ((s8[6291456]{0:T(1024)(128)(4,1)}), s8[4194304]{0:T(1024)(128)(4,1)S(1)}, s32[]{:S(2)}) async-start(s8[6291456]{0:T(1024)(128)(4,1)} %bitcast.172), calls=%async_computation.2 | async-start | bytes 8388608 | tf_op jit(solution)/shard_map/while
  130.9 20.4 %slice-start.1 = ((s8[6291456]{0:T(1024)(128)(4,1)}), s8[2097152]{0:T(1024)(128)(4,1)S(1)}, s32[]{:S(2)}) async-start(s8[6291456]{0:T(1024)(128)(4,1)} %bitcast.172), calls=%async_computation.3 | async-start | bytes 4194304 | tf_op jit(solution)/shard_map/while
  161.0 2.7 copy-start.2
  164.7 20.4 %slice-start = ((s8[6291456]{0:T(1024)(128)(4,1)}), s8[4194304]{0:T(1024)(128)(4,1)S(1)}, s32[]{:S(2)}) async-start(s8[6291456]{0:T(1024)(128)(4,1)} %bitcast.172), calls=%async_computation.2 | async-start | bytes 8388608 | tf_op jit(solution)/shard_map/while
  164.7 20.4 %slice-start.1 = ((s8[6291456]{0:T(1024)(128)(4,1)}), s8[2097152]{0:T(1024)(128)(4,1)S(1)}, s32[]{:S(2)}) async-start(s8[6291456]{0:T(1024)(128)(4,1)} %bitcast.172), calls=%async_computation.3 | async-start | bytes 4194304 | tf_op jit(solution)/shard_map/while
  194.8 2.7 copy-start.2
  198.6 20.4 %slice-start = ((s8[6291456]{0:T(1024)(128)(4,1)}), s8[4194304]{0:T(1024)(128)(4,1)S(1)}, s32[]{:S(2)}) async-start(s8[6291456]{0:T(1024)(128)(4,1)} %bitcast.172), calls=%async_computation.2 | async-start | bytes 8388608 | tf_op jit(solution)/shard_map/while
  198.6 20.4 %slice-start.1 = ((s8[6291456]{0:T(1024)(128)(4,1)}), s8[2097152]{0:T(1024)(128)(4,1)S(1)}, s32[]{:S(2)}) async-start(s8[6291456]{0:T(1024)(128)(4,1)} %bitcast.172), calls=%async_computation.3 | async-start | bytes 4194304 | tf_op jit(solution)/shard_map/while
  228.7 2.7 copy-start.2
  232.4 20.4 %slice-start = ((s8[6291456]{0:T(1024)(128)(4,1)}), s8[4194304]{0:T(1024)(128)(4,1)S(1)}, s32[]{:S(2)}) async-start(s8[6291456]{0:T(1024)(128)(4,1)} %bitcast.172), calls=%async_computation.2 | async-start | bytes 8388608 | tf_op jit(solution)/shard_map/while
  232.5 20.4 %slice-start.1 = ((s8[6291456]{0:T(1024)(128)(4,1)}), s8[2097152]{0:T(1024)(128)(4,1)S(1)}, s32[]{:S(2)}) async-start(s8[6291456]{0:T(1024)(128)(4,1)} %bitcast.172), calls=%async_computation.3 | async-start | bytes 4194304 | tf_op jit(solution)/shard_map/while
  262.6 2.7 copy-start.2
  266.3 20.4 %slice-start = ((s8[6291456]{0:T(1024)(128)(4,1)}), s8[4194304]{0:T(1024)(128)(4,1)S(1)}, s32[]{:S(2)}) async-start(s8[6291456]{0:T(1024)(128)(4,1)} %bitcast.172), calls=%async_computation.2 | async-start | bytes 8388608 | tf_op jit(solution)/shard_map/while
  266.3 20.4 %slice-start.1 = ((s8[6291456]{0:T(1024)(128)(4,1)}), s8[2097152]{0:T(1024)(128)(4,1)S(1)}, s32[]{:S(2)}) async-start(s8[6291456]{0:T(1024)(128)(4,1)} %bitcast.172), calls=%async_computation.3 | async-start | bytes 4194304 | tf_op jit(solution)/shard_map/while
  296.4 2.7 copy-start.2
  299.1 27.9 %all-to-all-start = ((bf16[32,8,192]{2,1,0:T(8,128)(2,1)}), bf16[32,8,192]{2,1,0:T(8,128)(2,1)S(1)}, u32[]{:S(2)}, u32[]{:S(2)}) async-start(bf16[32,8,192]{2,1,0:T(8,128)(2,1)} %reshape.180), calls=%async_computation | async-start | bytes 262144 | tf_op jit(solution)/shard_map/all_to_all | solution.py:64
  313.3 526.9 %collective-permute-start.2 = (f32[64,64,128]{2,1,0:T(8,128)}, f32[64,64,128]{2,1,0:T(8,128)}, u32[]{:S(2)}, u32[]{:S(2)}) collective-permute-start(f32[64,64,128]{2,1,0:T(8,128)} %bitcast.60), channel_id=1, source_target_pairs={{0,1},{1,2},{2,3},{4,5},{5,6},{6,7},{8,9},{9,10},{10,11},{12,13},{... | collective-permute-start | bytes 6291464 | tf_op jit(solution)/shard_map/ppermute | solution.py:12
  316.6 523.7 %collective-permute-start.3 = (f32[64,64,128]{2,1,0:T(8,128)}, f32[64,64,128]{2,1,0:T(8,128)}, u32[]{:S(2)}, u32[]{:S(2)}) collective-permute-start(f32[64,64,128]{2,1,0:T(8,128)} %bitcast.62), channel_id=1, source_target_pairs={{0,4},{4,8},{8,12},{12,16},{16,20},{20,24},{24,28},{1,5},{5,9},{9,... | collective-permute-start | bytes 6291464 | tf_op jit(solution)/shard_map/ppermute | solution.py:12
  840.3 6.0 copy-start.1
where the time goes:
time: 851 us; the launch traced here: 846 us
  local copies, waits for them, and re-layouts  397 us (47%)
  matrix products  342 us (40%)
  other arithmetic  80.1 us (9%)
  starting transfers between devices  25.9 us (3%)
    gather x8, local copies, waits for them, and re-layouts, far_block(): gathered = table[slots]  175 us
    convert_element_type x8, local copies, waits for them, and re-layouts, far_block(): pair_kernel(row_nodes[:, None].astype(jnp.float32), far_nodes)  167 us
    dot_general x8, matrix products, near_step(): jnp.einsum('jkab,jnb->jkna', kernel_block, dens_block, preferred_element_...  163 us
    dot_general x8, matrix products, far_block(): jnp.einsum('irn,irp->inp', far_coef, out_basis, preferred_element_type=jn...  94.7 us
    dot_general x8, matrix products, add_rows(): lax.dot_general(selector, partial_flat, (((0,), (0,)), ((), ())), precisi...  77.6 us
    convert_element_type x8, other arithmetic, far_block(): pair_kernel(row_nodes[:, None].astype(jnp.float32), far_nodes)  61.9 us
    while x48, local copies, waits for them, and re-layouts  21.3 us
  transfers between devices with their start and end apart: 6, of which 0 were waited for; matrix products, arithmetic and copies ran while one was open for 93% of the time, Pallas kernels for 0%

commit v1 on v0

v1 whole, which is shorter than its diff:
```python
import jax
import jax.numpy as jnp
from jax import lax
from jax.experimental import pallas as pl
from jax.experimental.pallas import tpu as pltpu
from jax.sharding import PartitionSpec as P

SOFTENING = 0.25
DEPTH = 16
GROUP = 8
VMEM_BYTES = 48 * 1024 * 1024
HALF_MATH = False


def passed_along(x, axis, by):
    length = lax.axis_size(axis)
    pairs = [(i, i + by) for i in range(length) if 0 <= i + by < length]
    return lax.ppermute(x, axis, pairs)


def whole(space=pltpu.VMEM):
    return pl.BlockSpec(memory_space=space)


def params():
    return pltpu.CompilerParams(vmem_limit_bytes=VMEM_BYTES)


def split_three(x):
    high = lax.reduce_precision(x, 8, 7)
    rest = x - high
    middle = lax.reduce_precision(rest, 8, 7)
    return [high, middle, rest - middle]


def as_targets(coords):
    x = coords.astype(jnp.float32)
    square = jnp.sum(x * x, axis=1, keepdims=True)
    ones = jnp.ones_like(square)
    rows = [x] + split_three(square) + [ones] * 3 + [jnp.zeros_like(square)] * (DEPTH - 9)
    return jnp.concatenate(rows, axis=1).astype(jnp.bfloat16)


def as_sources(coords):
    x = coords.astype(jnp.float32)
    square = jnp.sum(x * x, axis=1, keepdims=True) + SOFTENING
    ones = jnp.ones_like(square)
    rows = [-2.0 * x] + [ones] * 3 + split_three(square) + [jnp.zeros_like(square)] * (DEPTH - 9)
    return jnp.concatenate(rows, axis=1).astype(jnp.bfloat16)


def inverse_root(squared):
    if HALF_MATH:
        return lax.rsqrt(squared.astype(jnp.bfloat16))
    return lax.rsqrt(squared).astype(jnp.bfloat16)


def turned(block):
    return jnp.transpose(block.astype(jnp.float32)).astype(jnp.bfloat16)


def outgoing_kernel(send_ref, basis_ref, density_ref, out_ref, coef_ref):
    leaves, rank, _ = basis_ref.shape
    half = rank // 2

    def make(j, carry):
        coef = lax.dot_general(
            basis_ref[j], density_ref[j], (((1,), (1,)), ((), ())),
            preferred_element_type=jnp.float32,
        )
        coef_ref[j] = jnp.concatenate([coef[:half], coef[half:]], axis=1).astype(jnp.bfloat16)
        return carry

    lax.fori_loop(0, leaves, make, 0, unroll=4)

    def pick(q, carry):
        out_ref[q] = coef_ref[send_ref[q]]
        return carry

    lax.fori_loop(0, out_ref.shape[0], pick, 0, unroll=8)


def outgoing_blocks(send, basis_in, density):
    leaves, rank, _ = basis_in.shape
    fields = density.shape[1]
    shape = (rank // 2, 2 * fields)
    return pl.pallas_call(
        outgoing_kernel,
        out_shape=jax.ShapeDtypeStruct((send.shape[0],) + shape, jnp.bfloat16),
        in_specs=[whole(pltpu.SMEM), whole(), whole()],
        out_specs=whole(),
        scratch_shapes=[pltpu.VMEM((leaves,) + shape, jnp.bfloat16)],
        compiler_params=params(),
        name="outgoing",
    )(send, basis_in, density)


def near_kernel(codes_ref, sources_ref, targets_ref, density_ref, own_ref, deep_ref, wide_ref, acc_ref):
    leaves = sources_ref.shape[0]
    near = codes_ref.shape[1]
    width = sources_ref.shape[2]
    acc_ref[...] = jnp.zeros_like(acc_ref)

    def column(j, carry):
        source = turned(sources_ref[j])
        fields = density_ref[j]
        saved = []
        for first in range(0, near, 2):
            picks = [codes_ref[j, k] for k in range(first, min(first + 2, near))]
            tiles = [targets_ref[t] for t in picks]
            tile = tiles[0] if len(tiles) == 1 else jnp.concatenate(tiles, axis=1)
            squared = jnp.dot(source, tile, preferred_element_type=jnp.float32)
            block = inverse_root(squared)
            saved.append((picks, block))
        parts = [(p, jnp.dot(fields, b, preferred_element_type=jnp.float32)) for p, b in saved]
        for picks, part in parts:
            for place, t in enumerate(picks):
                acc_ref[t] += part[:, place * width:(place + 1) * width]
        return carry

    lax.fori_loop(0, leaves, column, 0)
    own_ref[...] = acc_ref[:leaves]
    deep_ref[...] = acc_ref[leaves:2 * leaves].astype(jnp.bfloat16)
    wide_ref[...] = acc_ref[2 * leaves:].astype(jnp.bfloat16)


def near_sums(codes, sources, targets, density):
    leaves, fields, width = density.shape
    pairs = leaves * codes.shape[1] * width * width
    return pl.pallas_call(
        near_kernel,
        out_shape=[
            jax.ShapeDtypeStruct(density.shape, jnp.float32),
            jax.ShapeDtypeStruct(density.shape, jnp.bfloat16),
            jax.ShapeDtypeStruct(density.shape, jnp.bfloat16),
        ],
        in_specs=[whole(pltpu.SMEM), whole(), whole(), whole()],
        out_specs=[whole(), whole(), whole()],
        scratch_shapes=[pltpu.VMEM((3 * leaves, fields, width), jnp.float32)],
        compiler_params=params(),
        cost_estimate=pl.CostEstimate(
            flops=pairs * 600, bytes_accessed=16 * 2**20, transcendentals=pairs
        ),
        name="near",
    )(codes, sources, targets, density)


def far_kernel(slots_ref, nodes_ref, far_nodes_ref, table_ref, basis_ref, out_ref):
    leaves, _, rank = nodes_ref.shape
    count = slots_ref.shape[1]
    half = rank // 2
    fields = table_ref.shape[2] // 2
    lanes = lax.broadcasted_iota(jnp.int32, (DEPTH, 4 * half), 1)

    def four(side, picks):
        tile = far_nodes_ref[picks[3], side]
        for place in (2, 1, 0):
            tile = jnp.where(lanes < (place + 1) * half, far_nodes_ref[picks[place], side], tile)
        return tile

    def row(i, carry):
        own = turned(nodes_ref[i])
        saved = []
        for first in range(0, count, GROUP):
            picks = [slots_ref[i, a] for a in range(first, first + GROUP)]
            coupling = []
            for side in range(2):
                tile = jnp.concatenate([four(side, picks[:4]), four(side, picks[4:])], axis=1)
                squared = jnp.dot(own, tile, preferred_element_type=jnp.float32)
                coupling.append(inverse_root(squared))
            saved.append((picks, jnp.concatenate(coupling, axis=0)))
        columns = jnp.concatenate([table_ref[s] for picks, _ in saved for s in picks], axis=0)
        total = jnp.dot(jnp.concatenate([b for _, b in saved], axis=1), columns, preferred_element_type=jnp.float32)
        far_coef = total[:rank, :fields] + total[rank:, fields:]
        out_ref[i] = jnp.dot(
            turned(far_coef), basis_ref[i], preferred_element_type=jnp.float32
        )
        return carry

    lax.fori_loop(0, leaves, row, 0, unroll=2)


def far_sums(slots, nodes, far_nodes, table, basis_out):
    leaves, rank, width = basis_out.shape
    fields = table.shape[2] // 2
    pairs = leaves * slots.shape[1] * rank * rank
    return pl.pallas_call(
        far_kernel,
        out_shape=jax.ShapeDtypeStruct((leaves, fields, width), jnp.float32),
        in_specs=[whole(pltpu.SMEM)] + [whole()] * 4,
        out_specs=whole(),
        compiler_params=params(),
        cost_estimate=pl.CostEstimate(
            flops=pairs * 600, bytes_accessed=8 * 2**20, transcendentals=pairs
        ),
        name="far",
    )(slots, nodes, far_nodes, table, basis_out)


def halves_repeated(far_nodes):
    half = far_nodes.shape[2] // 2
    sides = [jnp.concatenate([far_nodes[:, :, s * half:(s + 1) * half]] * 4, axis=2) for s in range(2)]
    return jnp.stack(sides, axis=1)


def shards(density, basis_in, basis_out, points, nodes, near_rows, send_leaf, adm_slot):
    leaves, fields, leaf_size = density.shape
    rank_size = basis_in.shape[1]
    deep_count = lax.axis_size("deep")
    devices = lax.axis_size("wide") * deep_count
    capacity = send_leaf.shape[2]
    axes = ("wide", "deep")
    send = send_leaf.reshape(devices * capacity)
    deep_points = passed_along(points, "deep", -1)
    wide_points = passed_along(points, "wide", -1)
    outgoing = outgoing_blocks(send, basis_in, density)
    outgoing = outgoing.reshape(devices, capacity * outgoing.shape[1], outgoing.shape[2])
    out_nodes = nodes.reshape(leaves, -1)[send].reshape(devices, capacity, 3 * rank_size)
    table_nodes = lax.all_to_all(out_nodes, axes, split_axis=0, concat_axis=0, tiled=True)
    table = lax.all_to_all(outgoing, axes, split_axis=0, concat_axis=0, tiled=True)
    table = table.reshape(devices * capacity, rank_size // 2, 2 * fields)
    far_nodes = as_targets(table_nodes.reshape(devices * capacity, 3, rank_size))
    far_nodes = halves_repeated(far_nodes)

    my_device = lax.axis_index("wide") * deep_count + lax.axis_index("deep")
    point_table = as_targets(jnp.concatenate([points, deep_points, wide_points], axis=0))
    offset = near_rows // leaves - my_device
    region = jnp.where(offset == 0, 0, jnp.where(offset == 1, 1, 2))
    codes = region * leaves + near_rows % leaves
    own, for_deep, for_wide = near_sums(codes, as_sources(points), point_table, density)
    from_deep = passed_along(for_deep, "deep", 1)
    from_wide = passed_along(for_wide, "wide", 1)
    far_field = far_sums(adm_slot, as_sources(nodes), far_nodes, table, basis_out)
    return far_field + (own + from_deep.astype(jnp.float32) + from_wide.astype(jnp.float32))


def solution(mesh):
    split = ("wide", "deep")
    in_specs = (
        P(split, None, None),
        P(split, None, None),
        P(split, None, None),
        P(split, None, None),
        P(split, None, None),
        P(split, None),
        P(split, None, None),
        P(split, None),
    )
    return jax.shard_map(
        shards, mesh=mesh, in_specs=in_specs, out_specs=P(split, None, None), check_vma=False
    )
```

time: 851 us -> 152 us (0.18)
  local copies, waits for them, and re-layouts: 397 us -> 14.3 us
  matrix products: 342 us -> 0 us
  Pallas kernels: 0 us -> 101 us
  other arithmetic: 80.1 us -> 9.78 us
    dot_general x41 -> x0, matrix products: 342 us -> none  [the longest x8 163 us: near_step(): jnp.einsum('jkab,jnb->jkna', kernel_block, dens_block, preferred_element_...]
    gather x11 -> x1, local copies, waits for them, and re-layouts: 179 us -> 1.79 us  [shards(): nodes.reshape(leaves, -1)[send].reshape(devices, capacity, 3 * rank_size)]
    convert_element_type x8 -> x1, local copies, waits for them, and re-layouts: 167 us -> 0.11 us  [as_targets(): x = coords.astype(jnp.float32)]
    pallas_call x0 -> x3, Pallas kernels: none -> 101 us  [the longest x1 51.6 us: far_sums(): pl.pallas_call(far_kernel, out_shape=jax.ShapeDtypeStruct((leaves, fields...]
    convert_element_type x24 -> x2, other arithmetic: 67.6 us -> 0.82 us  [as_sources(): x = coords.astype(jnp.float32)]
    while x48 -> x0, local copies, waits for them, and re-layouts: 21.3 us -> none
    reshape x11 -> x3, local copies, waits for them, and re-layouts: 16.1 us -> 0.27 us  [the longest x2 0.17 us: shards(): send = send_leaf.reshape(devices * capacity)]
  transfers between devices with their start and end apart: 6 -> 6, of which waited for: 0 -> 1; matrix products, arithmetic and copies ran while one was open for 93% -> 12% of each run, Pallas kernels for 0% -> 67%
where the time goes in v1:
time: 152 us; the launch traced here: 151 us
  Pallas kernels  101 us (66%)
  starting transfers between devices  25.1 us (17%)
  local copies, waits for them, and re-layouts  14.3 us (9%)
  other arithmetic  9.78 us (6%)
    pallas_call x1, Pallas kernels, far_sums(): pl.pallas_call(far_kernel, out_shape=jax.ShapeDtypeStruct((leaves, fields...  51.6 us
    pallas_call x1, Pallas kernels, near_sums(): pl.pallas_call(near_kernel, out_shape=[jax.ShapeDtypeStruct(density.shape...  43.5 us
    ppermute x4, starting transfers between devices, passed_along(): return lax.ppermute(x, axis, pairs)  10.2 us
    all_to_all x1, starting transfers between devices, shards(): lax.all_to_all(out_nodes, axes, split_axis=0, concat_axis=0, tiled=True)  9.09 us
    concatenate x6, local copies, waits for them, and re-layouts, as_targets(): return jnp.concatenate(rows, axis=1).astype(jnp.bfloat16)  7.09 us
    pallas_call x1, Pallas kernels, outgoing_blocks(): pl.pallas_call(outgoing_kernel, out_shape=jax.ShapeDtypeStruct((send.shap...  6.07 us
    all_to_all x1, starting transfers between devices, shards(): lax.all_to_all(outgoing, axes, split_axis=0, concat_axis=0, tiled=True)  5.8 us
    unnamed x19, local copies, waits for them, and re-layouts  3.82 us
  transfers between devices with their start and end apart: 6, of which 1 were waited for; matrix products, arithmetic and copies ran while one was open for 12% of the time, Pallas kernels for 67%

profile of v1, /device:TPU:0, one launch (start us, length us, event | category | flops | bytes accessed | tf_op | source)
XLA Modules:
  0.0 150.8 jit_solution(5774018280682597638)
XLA Ops:
  0.0 1.0 fusion.10
  1.0 1.3 collective-permute-start
  2.3 1.3 collective-permute-start.1
  3.6 0.8 copy.36
  4.4 0.1 reshape.173
  4.5 0.9 copy.35
  5.4 0.1 copy.37
  5.5 1.8 %gather_fusion = bf16[256,192]{1,0:T(8,128)(2,1)} fusion(bf16[64,192]{1,0:T(8,128)(2,1)S(1)} %copy.37, s32[1024]{0:T(1024)S(1)} %pad_clamp_fusion), kind=kCustom, calls=%fused_computation | custom fusion | bytes 197632 | tf_op jit(solution)/shard_map/gather | solution.py:218
  7.3 9.1 %all-to-all-start = ((bf16[32,8,192]{2,1,0:T(8,128)(2,1)}), bf16[32,8,192]{2,1,0:T(8,128)(2,1)S(1)}, u32[]{:S(2)}, u32[]{:S(2)}) async-start(bf16[32,8,192]{2,1,0:T(8,128)(2,1)} %bitcast.3), calls=%async_computation | async-start | bytes 262144 | tf_op jit(solution)/shard_map/all_to_all | solution.py:219
  16.4 0.8 multiply_reduce_fusion.3
  17.2 0.8 convert_element_type.25
  18.0 0.1 reshape.175.send_ref
  18.2 0.1 fusion.4
  18.3 0.1 copy.40
  18.4 6.1 %outgoing.1 = bf16[256,32,128]{2,1,0:T(8,128)(2,1)} custom-call(s32[256]{0:T(256)S(1)} %reshape.175.send_ref, bf16[64,64,128]{2,1,0:T(8,128)(2,1)S(1)} %copy-done, bf16[64,64,128]{2,1,0:T(8,128)(2,1)S(1)} %copy-done.1), custom_call_target="tpu_custom_call" | custom-call | tf_op jit(solution)/shard_map/outgoing/pallas_call | solution.py:87
  24.4 0.2 all-to-all-done
  24.6 5.8 %all-to-all-start.1 = ((bf16[32,256,128]{2,1,0:T(8,128)(2,1)}), bf16[32,256,128]{2,1,0:T(8,128)(2,1)}, u32[]{:S(2)}, u32[]{:S(2)}) async-start(bf16[32,256,128]{2,1,0:T(8,128)(2,1)} %bitcast.8), calls=%async_computation.1 | async-start | bytes 4194304 | tf_op jit(solution)/shard_map/all_to_all | solution.py:220
  30.4 0.1 fusion.5
  30.5 0.1 fusion.2
  30.6 0.1 fusion.1
  30.8 0.3 concatenate.51.nodes_ref
  31.1 0.3 concatenate.59.sources_ref
  31.4 0.0 collective-permute-done
  31.5 0.0 collective-permute-done.1
  31.5 0.3 multiply_reduce_fusion.1
  31.8 0.8 fusion.3
  32.6 0.1 concatenate.62
  32.7 0.1 concatenate.61
  32.8 3.7 %concatenate.63.targets_ref = bf16[192,16,128]{2,1,0:T(8,128)(2,1)S(1)} concatenate(bf16[192,3,128]{2,1,0:T(4,128)(2,1)S(1)} %constant_dynamic-update-slice_fusion, bf16[192,1,128]{2,1,0:T(2,128)(2,1)} %get-tuple-element.18, bf16[192,1,128]{2,1,0:T(2,128)(2,1)S(1)} %get-tuple-element.17, bf16[192,1,128]{2,1,0:T(2,128)(2,1)S(1)} %get-tuple-element.16, ...), dimensions={1} | concatenate | bytes 1572864 | tf_op jit(solution)/shard_map/concatenate | solution.py:41
  36.4 43.5 %near.1 = (f32[64,64,128]{2,1,0:T(8,128)}, bf16[64,64,128]{2,1,0:T(8,128)(2,1)}, bf16[64,64,128]{2,1,0:T(8,128)(2,1)}) custom-call(s32[64,27]{1,0:T(8,128)S(1)} %fusion.7.codes_ref, bf16[64,16,128]{2,1,0:T(8,128)(2,1)S(1)} %concatenate.59.sources_ref, bf16[192,16,128]{2,1,0:T(8,128)(2,1)S(1)} %concatenate.63.targets_ref, bf16[64,64,128]{2,1,0:T(8,128)(2,1)S(1)} %copy-done.1), custom_call_target="tpu_custom_call" | custom-call | flops 16986931200 | bytes 16777216 | tf_op jit(solution)/shard_map/near/pallas_call | solution.py:130
  79.9 3.1 %collective-permute-start.2 = (bf16[64,64,128]{2,1,0:T(8,128)(2,1)}, bf16[64,64,128]{2,1,0:T(8,128)(2,1)}, u32[]{:S(2)}, u32[]{:S(2)}) collective-permute-start(bf16[64,64,128]{2,1,0:T(8,128)(2,1)} %get-tuple-element.9), channel_id=1, source_target_pairs={{0,1},{1,2},{2,3},{4,5},{5,6},{6,7},{8,9},{9,10},{10,11},{12,13},{... | collective-permute-start | bytes 3145736 | tf_op jit(solution)/shard_map/ppermute | solution.py:18
  83.0 4.6 %collective-permute-start.3 = (bf16[64,64,128]{2,1,0:T(8,128)(2,1)}, bf16[64,64,128]{2,1,0:T(8,128)(2,1)}, u32[]{:S(2)}, u32[]{:S(2)}) collective-permute-start(bf16[64,64,128]{2,1,0:T(8,128)(2,1)} %get-tuple-element.10), channel_id=1, source_target_pairs={{0,4},{4,8},{8,12},{12,16},{16,20},{20,24},{24,28},{1,5},{5,9},{9,... | collective-permute-start | bytes 3145736 | tf_op jit(solution)/shard_map/ppermute | solution.py:18
  87.6 0.1 convert_element_type.26
  87.7 0.4 multiply_reduce_fusion
  88.1 0.3 fusion
  88.4 0.1 concatenate.53
  88.4 0.1 concatenate.52
  88.5 3.2 %concatenate.54 = bf16[256,16,64]{2,1,0:T(8,128)(2,1)S(1)} concatenate(bf16[256,3,64]{2,1,0:T(4,128)(2,1)S(1)} %convert_element_type.26, bf16[256,1,64]{2,1,0:T(2,128)(2,1)S(1)} %get-tuple-element.15, bf16[256,1,64]{2,1,0:T(2,128)(2,1)S(1)} %get-tuple-element.14, bf16[256,1,64]{2,1,0:T(2,128)(2,1)S(1)} %get-tuple-element.13, bf16[256,3,64]{2,1,0:T(4,128)(2,1)S(1)} %concatenate.52, ...), dimensions={1} | concatenate | bytes 1048576 | tf_op jit(solution)/shard_map/concatenate | solution.py:41
  91.7 0.5 fusion.9
  92.2 2.1 %maximum_bitcast_fusion = (bf16[256,1,16,128]{3,2,1,0:T(8,128)(2,1)S(1)}, bf16[256,1,16,128]{3,2,1,0:T(8,128)(2,1)S(1)}) fusion(bf16[256,16,32]{2,1,0:T(8,128)(2,1)S(1)} %get-tuple-element.11, bf16[256,16,32]{2,1,0:T(8,128)(2,1)S(1)} %get-tuple-element.12), kind=kLoop, calls=%fused_computation.3 | loop fusion | flops 8388608 | bytes 2621440 | tf_op jit(solution)/shard_map/stack | solution.py:203
  94.3 0.0 copy-start.2
  94.3 0.0 copy-start.3
  94.4 0.2 pad_maximum_fusion.far_nodes_ref
  94.6 1.0 copy-done.2
  95.6 51.6 %far.1 = f32[64,64,128]{2,1,0:T(8,128)S(1)} custom-call(s32[64,96]{1,0:T(8,128)S(1)} %copy-done.3, bf16[64,16,64]{2,1,0:T(8,128)(2,1)S(1)} %concatenate.51.nodes_ref, bf16[256,2,16,128]{3,2,1,0:T(8,128)(2,1)S(1)} %pad_maximum_fusion.far_nodes_ref, bf16[256,32,128]{2,1,0:T(8,128)(2,1)} %bitcast.9.table_ref, bf16[64,64,128]{2,1,0:T(8,128)(2,1)S(1)} %copy-done.2), custom_call_target="tpu_custom_call" | custom-call | flops 15099494400 | bytes 8388608 | tf_op jit(solution)/shard_map/far/pallas_call | solution.py:187
  147.1 0.0 collective-permute-done.2
  147.1 0.0 collective-permute-done.3
  147.2 3.7 %add_add_fusion = f32[64,64,128]{2,1,0:T(8,128)} fusion(f32[64,64,128]{2,1,0:T(8,128)S(1)} %far.1, bf16[64,64,128]{2,1,0:T(8,128)(2,1)} %collective-permute-done.3, f32[64,64,128]{2,1,0:T(8,128)S(1)} %copy-done.4, bf16[64,64,128]{2,1,0:T(8,128)(2,1)} %collective-permute-done.2), kind=kLoop, calls=%fused_computation.2 | loop fusion | flops 2621440 | bytes 8388608 | tf_op jit(solution)/shard_map/add | solution.py:234
  (25 shorter events, 0.3 us)
Async XLA Ops:
  0.0 18.1 %copy-start.5 = (bf16[64,3,128]{2,0,1:T(8,128)(2,1)S(1)}, bf16[64,3,128]{2,0,1:T(8,128)(2,1)}, u32[]{:S(2)}) copy-start(bf16[64,3,128]{2,0,1:T(8,128)(2,1)} %param.11) | copy-start | bytes 147460
  0.0 18.2 %copy-start.6 = (s32[64,27]{0,1:T(8,128)S(1)}, s32[64,27]{0,1:T(8,128)}, u32[]{:S(2)}) copy-start(s32[64,27]{0,1:T(8,128)} %param.13) | copy-start | bytes 20740
  0.0 18.3 %copy-start.1 = (bf16[64,64,128]{2,1,0:T(8,128)(2,1)S(1)}, bf16[64,64,128]{2,1,0:T(8,128)(2,1)}, u32[]{:S(2)}) copy-start(bf16[64,64,128]{2,1,0:T(8,128)(2,1)} %density_ref.3) | copy-start | bytes 3145732
  0.0 18.3 %copy-start = (bf16[64,64,128]{2,1,0:T(8,128)(2,1)S(1)}, bf16[64,64,128]{2,1,0:T(8,128)(2,1)}, u32[]{:S(2)}) copy-start(bf16[64,64,128]{2,1,0:T(8,128)(2,1)} %basis_ref.2) | copy-start | bytes 3145732
  1.0 30.4 %collective-permute-start = (bf16[64,3,128]{2,1,0:T(4,128)(2,1)S(1)}, bf16[64,3,128]{2,1,0:T(4,128)(2,1)S(1)}, u32[]{:S(2)}, u32[]{:S(2)}) collective-permute-start(bf16[64,3,128]{2,1,0:T(4,128)(2,1)S(1)} %get-tuple-element.19), channel_id=1, source_target_pairs={{1,0},{2,1},{3,2},{5,4},{6,5},{7,6},{9,8},{10,9},{11,10},{13,12},{... | collective-permute-start | bytes 147464 | tf_op jit(solution)/shard_map/ppermute | solution.py:18
  2.3 29.2 %collective-permute-start.1 = (bf16[64,3,128]{2,1,0:T(4,128)(2,1)S(1)}, bf16[64,3,128]{2,1,0:T(4,128)(2,1)S(1)}, u32[]{:S(2)}, u32[]{:S(2)}) collective-permute-start(bf16[64,3,128]{2,1,0:T(4,128)(2,1)S(1)} %get-tuple-element.19), channel_id=1, source_target_pairs={{4,0},{8,4},{12,8},{16,12},{20,16},{24,20},{28,24},{5,1},{9,5},{13... | collective-permute-start | bytes 147464 | tf_op jit(solution)/shard_map/ppermute | solution.py:18
  7.3 17.3 %all-to-all-start = ((bf16[32,8,192]{2,1,0:T(8,128)(2,1)}), bf16[32,8,192]{2,1,0:T(8,128)(2,1)S(1)}, u32[]{:S(2)}, u32[]{:S(2)}) async-start(bf16[32,8,192]{2,1,0:T(8,128)(2,1)} %bitcast.3), calls=%async_computation | async-start | bytes 262144 | tf_op jit(solution)/shard_map/all_to_all | solution.py:219
  24.6 69.9 %all-to-all-start.1 = ((bf16[32,256,128]{2,1,0:T(8,128)(2,1)}), bf16[32,256,128]{2,1,0:T(8,128)(2,1)}, u32[]{:S(2)}, u32[]{:S(2)}) async-start(bf16[32,256,128]{2,1,0:T(8,128)(2,1)} %bitcast.8), calls=%async_computation.1 | async-start | bytes 4194304 | tf_op jit(solution)/shard_map/all_to_all | solution.py:220
  79.9 67.2 %collective-permute-start.2 = (bf16[64,64,128]{2,1,0:T(8,128)(2,1)}, bf16[64,64,128]{2,1,0:T(8,128)(2,1)}, u32[]{:S(2)}, u32[]{:S(2)}) collective-permute-start(bf16[64,64,128]{2,1,0:T(8,128)(2,1)} %get-tuple-element.9), channel_id=1, source_target_pairs={{0,1},{1,2},{2,3},{4,5},{5,6},{6,7},{8,9},{9,10},{10,11},{12,13},{... | collective-permute-start | bytes 3145736 | tf_op jit(solution)/shard_map/ppermute | solution.py:18
  83.0 64.1 %collective-permute-start.3 = (bf16[64,64,128]{2,1,0:T(8,128)(2,1)}, bf16[64,64,128]{2,1,0:T(8,128)(2,1)}, u32[]{:S(2)}, u32[]{:S(2)}) collective-permute-start(bf16[64,64,128]{2,1,0:T(8,128)(2,1)} %get-tuple-element.10), channel_id=1, source_target_pairs={{0,4},{4,8},{8,12},{12,16},{16,20},{20,24},{24,28},{1,5},{5,9},{9,... | collective-permute-start | bytes 3145736 | tf_op jit(solution)/shard_map/ppermute | solution.py:18
  94.3 1.2 copy-start.2
  94.3 1.2 copy-start.3
  95.6 51.6 %copy-start.4 = (f32[64,64,128]{2,1,0:T(8,128)S(1)}, f32[64,64,128]{2,1,0:T(8,128)}, u32[]{:S(2)}) copy-start(f32[64,64,128]{2,1,0:T(8,128)} %get-tuple-element.8) | copy-start | bytes 6291460

commit v2 on v1

--- a/solution.py
+++ b/solution.py
@@ -10,6 +10,10 @@
 GROUP = 8
 VMEM_BYTES = 48 * 1024 * 1024
 HALF_MATH = False
+NEAR_TOGETHER = 4
+NEAR_LAG = 10
+FAR_TOGETHER = 4
+FAR_LAG = 10
 
 
 def passed_along(x, axis, by):
@@ -101,24 +105,31 @@
     width = sources_ref.shape[2]
     acc_ref[...] = jnp.zeros_like(acc_ref)
 
-    def column(j, carry):
-        source = turned(sources_ref[j])
-        fields = density_ref[j]
-        saved = []
-        for first in range(0, near, 2):
-            picks = [codes_ref[j, k] for k in range(first, min(first + 2, near))]
-            tiles = [targets_ref[t] for t in picks]
-            tile = tiles[0] if len(tiles) == 1 else jnp.concatenate(tiles, axis=1)
-            squared = jnp.dot(source, tile, preferred_element_type=jnp.float32)
-            block = inverse_root(squared)
-            saved.append((picks, block))
-        parts = [(p, jnp.dot(fields, b, preferred_element_type=jnp.float32)) for p, b in saved]
-        for picks, part in parts:
+    def columns(step, carry):
+        first_leaf = step * NEAR_TOGETHER
+        waiting = []
+
+        def apply(leaf, picks, block):
+            part = jnp.dot(density_ref[leaf], block, preferred_element_type=jnp.float32)
             for place, t in enumerate(picks):
                 acc_ref[t] += part[:, place * width:(place + 1) * width]
-        return carry
-
-    lax.fori_loop(0, leaves, column, 0)
+
+        for ahead in range(NEAR_TOGETHER):
+            j = first_leaf + ahead
+            source = turned(sources_ref[j])
+            for first in range(0, near, 2):
+                picks = [codes_ref[j, k] for k in range(first, min(first + 2, near))]
+                tiles = [targets_ref[t] for t in picks]
+                tile = tiles[0] if len(tiles) == 1 else jnp.concatenate(tiles, axis=1)
+                squared = jnp.dot(source, tile, preferred_element_type=jnp.float32)
+                waiting.append((j, picks, inverse_root(squared)))
+                if len(waiting) > NEAR_LAG:
+                    apply(*waiting.pop(0))
+        for item in waiting:
+            apply(*item)
+        return carry
+
+    lax.fori_loop(0, leaves // NEAR_TOGETHER, columns, 0)
     own_ref[...] = acc_ref[:leaves]
     deep_ref[...] = acc_ref[leaves:2 * leaves].astype(jnp.bfloat16)
     wide_ref[...] = acc_ref[2 * leaves:].astype(jnp.bfloat16)
@@ -158,26 +169,42 @@
             tile = jnp.where(lanes < (place + 1) * half, far_nodes_ref[picks[place], side], tile)
         return tile
 
-    def row(i, carry):
-        own = turned(nodes_ref[i])
-        saved = []
-        for first in range(0, count, GROUP):
-            picks = [slots_ref[i, a] for a in range(first, first + GROUP)]
-            coupling = []
-            for side in range(2):
-                tile = jnp.concatenate([four(side, picks[:4]), four(side, picks[4:])], axis=1)
-                squared = jnp.dot(own, tile, preferred_element_type=jnp.float32)
-                coupling.append(inverse_root(squared))
-            saved.append((picks, jnp.concatenate(coupling, axis=0)))
-        columns = jnp.concatenate([table_ref[s] for picks, _ in saved for s in picks], axis=0)
-        total = jnp.dot(jnp.concatenate([b for _, b in saved], axis=1), columns, preferred_element_type=jnp.float32)
-        far_coef = total[:rank, :fields] + total[rank:, fields:]
-        out_ref[i] = jnp.dot(
-            turned(far_coef), basis_ref[i], preferred_element_type=jnp.float32
-        )
-        return carry
-
-    lax.fori_loop(0, leaves, row, 0, unroll=2)
+    def rows(step, carry):
+        first_leaf = step * FAR_TOGETHER
+        waiting = []
+        totals = {}
+
+        def apply(ahead, picks, block):
+            columns = jnp.concatenate([table_ref[s] for s in picks], axis=0)
+            part = jnp.dot(block, columns, preferred_element_type=jnp.float32)
+            totals[ahead] = totals[ahead] + part if ahead in totals else part
+
+        def finish(ahead):
+            total = totals[ahead]
+            far_coef = total[:rank, :fields] + total[rank:, fields:]
+            i = first_leaf + ahead
+            out_ref[i] = jnp.dot(turned(far_coef), basis_ref[i], preferred_element_type=jnp.float32)
+
+        for ahead in range(FAR_TOGETHER):
+            i = first_leaf + ahead
+            own = turned(nodes_ref[i])
+            for first in range(0, count, GROUP):
+                picks = [slots_ref[i, a] for a in range(first, first + GROUP)]
+                coupling = []
+                for side in range(2):
+                    tile = jnp.concatenate([four(side, picks[:4]), four(side, picks[4:])], axis=1)
+                    squared = jnp.dot(own, tile, preferred_element_type=jnp.float32)
+                    coupling.append(inverse_root(squared))
+                waiting.append((ahead, picks, jnp.concatenate(coupling, axis=0)))
+                if len(waiting) > FAR_LAG:
+                    apply(*waiting.pop(0))
+        for item in waiting:
+            apply(*item)
+        for ahead in range(FAR_TOGETHER):
+            finish(ahead)
+        return carry
+
+    lax.fori_loop(0, leaves // FAR_TOGETHER, rows, 0)
 
 
 def far_sums(slots, nodes, far_nodes, table, basis_out):

time: 152 us -> 123 us (0.81)
  Pallas kernels: 101 us -> 72.5 us
    pallas_call x1, Pallas kernels: 51.6 us -> 36.4 us  [far_sums(): pl.pallas_call(far_kernel, out_shape=jax.ShapeDtypeStruct((leaves, fields...]
    pallas_call x1, Pallas kernels: 43.5 us -> 30 us  [near_sums(): pl.pallas_call(near_kernel, out_shape=[jax.ShapeDtypeStruct(density.shape...]
  transfers between devices with their start and end apart: 6 -> 6, of which waited for: 1 -> 1; matrix products, arithmetic and copies ran while one was open for 12% -> 15% of each run, Pallas kernels for 67% -> 59%
where the time goes in v2:
time: 123 us; the launch traced here: 122 us
  Pallas kernels  72.5 us (59%)
  starting transfers between devices  25.1 us (20%)
  local copies, waits for them, and re-layouts  14.3 us (12%)
  other arithmetic  9.78 us (8%)
    pallas_call x1, Pallas kernels, far_sums(): pl.pallas_call(far_kernel, out_shape=jax.ShapeDtypeStruct((leaves, fields...  36.4 us
    pallas_call x1, Pallas kernels, near_sums(): pl.pallas_call(near_kernel, out_shape=[jax.ShapeDtypeStruct(density.shape...  30 us
    ppermute x4, starting transfers between devices, passed_along(): return lax.ppermute(x, axis, pairs)  10.2 us
    all_to_all x1, starting transfers between devices, shards(): lax.all_to_all(out_nodes, axes, split_axis=0, concat_axis=0, tiled=True)  9.09 us
    concatenate x6, local copies, waits for them, and re-layouts, as_targets(): return jnp.concatenate(rows, axis=1).astype(jnp.bfloat16)  7.09 us
    pallas_call x1, Pallas kernels, outgoing_blocks(): pl.pallas_call(outgoing_kernel, out_shape=jax.ShapeDtypeStruct((send.shap...  6.07 us
    all_to_all x1, starting transfers between devices, shards(): lax.all_to_all(outgoing, axes, split_axis=0, concat_axis=0, tiled=True)  5.8 us
    unnamed x19, local copies, waits for them, and re-layouts  3.82 us
  transfers between devices with their start and end apart: 6, of which 1 were waited for; matrix products, arithmetic and copies ran while one was open for 15% of the time, Pallas kernels for 59%

profile of v2, /device:TPU:0, one launch (start us, length us, event | category | flops | bytes accessed | tf_op | source)
XLA Modules:
  0.0 122.2 jit_solution(9275256816497552968)
XLA Ops:
  0.0 1.0 fusion.10
  1.0 1.3 %collective-permute-start = (bf16[64,3,128]{2,1,0:T(4,128)(2,1)S(1)}, bf16[64,3,128]{2,1,0:T(4,128)(2,1)S(1)}, u32[]{:S(2)}, u32[]{:S(2)}) collective-permute-start(bf16[64,3,128]{2,1,0:T(4,128)(2,1)S(1)} %get-tuple-element.19), channel_id=1, source_target_pairs={{1,0},{2,1},{3,2},{5,4},{6,5},{7,6},{9,8},{10,9},{11,10},{13,12},{... | collective-permute-start | bytes 147464 | tf_op jit(solution)/shard_map/ppermute | solution.py:22
  2.3 1.3 %collective-permute-start.1 = (bf16[64,3,128]{2,1,0:T(4,128)(2,1)S(1)}, bf16[64,3,128]{2,1,0:T(4,128)(2,1)S(1)}, u32[]{:S(2)}, u32[]{:S(2)}) collective-permute-start(bf16[64,3,128]{2,1,0:T(4,128)(2,1)S(1)} %get-tuple-element.19), channel_id=1, source_target_pairs={{4,0},{8,4},{12,8},{16,12},{20,16},{24,20},{28,24},{5,1},{9,5},{13... | collective-permute-start | bytes 147464 | tf_op jit(solution)/shard_map/ppermute | solution.py:22
  3.6 0.8 copy.36
  4.4 0.1 reshape.173
  4.5 0.9 copy.35
  5.4 0.1 copy.37
  5.5 1.8 %gather_fusion = bf16[256,192]{1,0:T(8,128)(2,1)} fusion(bf16[64,192]{1,0:T(8,128)(2,1)S(1)} %copy.37, s32[1024]{0:T(1024)S(1)} %pad_clamp_fusion), kind=kCustom, calls=%fused_computation | custom fusion | bytes 197632 | tf_op jit(solution)/shard_map/gather | solution.py:245
  7.3 9.1 %all-to-all-start = ((bf16[32,8,192]{2,1,0:T(8,128)(2,1)}), bf16[32,8,192]{2,1,0:T(8,128)(2,1)S(1)}, u32[]{:S(2)}, u32[]{:S(2)}) async-start(bf16[32,8,192]{2,1,0:T(8,128)(2,1)} %bitcast.3), calls=%async_computation | async-start | bytes 262144 | tf_op jit(solution)/shard_map/all_to_all | solution.py:246
  16.4 0.8 multiply_reduce_fusion.3
  17.2 0.8 convert_element_type.25
  18.0 0.1 reshape.175.send_ref
  18.2 0.1 fusion.4
  18.3 0.1 copy.40
  18.4 6.1 %outgoing.1 = bf16[256,32,128]{2,1,0:T(8,128)(2,1)} custom-call(s32[256]{0:T(256)S(1)} %reshape.175.send_ref, bf16[64,64,128]{2,1,0:T(8,128)(2,1)S(1)} %copy-done, bf16[64,64,128]{2,1,0:T(8,128)(2,1)S(1)} %copy-done.1), custom_call_target="tpu_custom_call" | custom-call | tf_op jit(solution)/shard_map/outgoing/pallas_call | solution.py:91
  24.4 0.2 all-to-all-done
  24.6 5.8 %all-to-all-start.1 = ((bf16[32,256,128]{2,1,0:T(8,128)(2,1)}), bf16[32,256,128]{2,1,0:T(8,128)(2,1)}, u32[]{:S(2)}, u32[]{:S(2)}) async-start(bf16[32,256,128]{2,1,0:T(8,128)(2,1)} %bitcast.8), calls=%async_computation.1 | async-start | bytes 4194304 | tf_op jit(solution)/shard_map/all_to_all | solution.py:247
  30.4 0.1 fusion.5
  30.5 0.1 fusion.2
  30.6 0.1 fusion.1
  30.8 0.3 concatenate.51.nodes_ref
  31.1 0.3 concatenate.59.sources_ref
  31.4 0.0 collective-permute-done
  31.5 0.3 multiply_reduce_fusion.1
  31.8 0.8 fusion.3
  32.6 0.1 concatenate.62
  32.7 0.1 concatenate.61
  32.7 3.7 %concatenate.63.targets_ref = bf16[192,16,128]{2,1,0:T(8,128)(2,1)S(1)} concatenate(bf16[192,3,128]{2,1,0:T(4,128)(2,1)S(1)} %constant_dynamic-update-slice_fusion, bf16[192,1,128]{2,1,0:T(2,128)(2,1)} %get-tuple-element.18, bf16[192,1,128]{2,1,0:T(2,128)(2,1)S(1)} %get-tuple-element.17, bf16[192,1,128]{2,1,0:T(2,128)(2,1)S(1)} %get-tuple-element.16, ...), dimensions={1} | concatenate | bytes 1572864 | tf_op jit(solution)/shard_map/concatenate | solution.py:45
  36.4 30.0 %near.1 = (f32[64,64,128]{2,1,0:T(8,128)}, bf16[64,64,128]{2,1,0:T(8,128)(2,1)}, bf16[64,64,128]{2,1,0:T(8,128)(2,1)}) custom-call(s32[64,27]{1,0:T(8,128)S(1)} %fusion.7.codes_ref, bf16[64,16,128]{2,1,0:T(8,128)(2,1)S(1)} %concatenate.59.sources_ref, bf16[192,16,128]{2,1,0:T(8,128)(2,1)S(1)} %concatenate.63.targets_ref, bf16[64,64,128]{2,1,0:T(8,128)(2,1)S(1)} %copy-done.1), custom_call_target="tpu_custom_call" | custom-call | flops 16986931200 | bytes 16777216 | tf_op jit(solution)/shard_map/near/pallas_call | solution.py:141
  66.4 3.1 %collective-permute-start.2 = (bf16[64,64,128]{2,1,0:T(8,128)(2,1)}, bf16[64,64,128]{2,1,0:T(8,128)(2,1)}, u32[]{:S(2)}, u32[]{:S(2)}) collective-permute-start(bf16[64,64,128]{2,1,0:T(8,128)(2,1)} %get-tuple-element.9), channel_id=1, source_target_pairs={{0,1},{1,2},{2,3},{4,5},{5,6},{6,7},{8,9},{9,10},{10,11},{12,13},{... | collective-permute-start | bytes 3145736 | tf_op jit(solution)/shard_map/ppermute | solution.py:22
  69.5 4.6 %collective-permute-start.3 = (bf16[64,64,128]{2,1,0:T(8,128)(2,1)}, bf16[64,64,128]{2,1,0:T(8,128)(2,1)}, u32[]{:S(2)}, u32[]{:S(2)}) collective-permute-start(bf16[64,64,128]{2,1,0:T(8,128)(2,1)} %get-tuple-element.10), channel_id=1, source_target_pairs={{0,4},{4,8},{8,12},{12,16},{16,20},{20,24},{24,28},{1,5},{5,9},{9,... | collective-permute-start | bytes 3145736 | tf_op jit(solution)/shard_map/ppermute | solution.py:22
  74.1 0.1 convert_element_type.26
  74.2 0.4 multiply_reduce_fusion
  74.6 0.3 fusion
  74.9 0.1 concatenate.53
  75.0 0.1 concatenate.52
  75.0 3.2 %concatenate.54 = bf16[256,16,64]{2,1,0:T(8,128)(2,1)S(1)} concatenate(bf16[256,3,64]{2,1,0:T(4,128)(2,1)S(1)} %convert_element_type.26, bf16[256,1,64]{2,1,0:T(2,128)(2,1)S(1)} %get-tuple-element.15, bf16[256,1,64]{2,1,0:T(2,128)(2,1)S(1)} %get-tuple-element.14, bf16[256,1,64]{2,1,0:T(2,128)(2,1)S(1)} %get-tuple-element.13, bf16[256,3,64]{2,1,0:T(4,128)(2,1)S(1)} %concatenate.52, ...), dimensions={1} | concatenate | bytes 1048576 | tf_op jit(solution)/shard_map/concatenate | solution.py:45
  78.2 0.5 fusion.9
  78.7 2.1 %maximum_bitcast_fusion = (bf16[256,1,16,128]{3,2,1,0:T(8,128)(2,1)S(1)}, bf16[256,1,16,128]{3,2,1,0:T(8,128)(2,1)S(1)}) fusion(bf16[256,16,32]{2,1,0:T(8,128)(2,1)S(1)} %get-tuple-element.11, bf16[256,16,32]{2,1,0:T(8,128)(2,1)S(1)} %get-tuple-element.12), kind=kLoop, calls=%fused_computation.3 | loop fusion | flops 8388608 | bytes 2621440 | tf_op jit(solution)/shard_map/stack | solution.py:230
  80.9 0.0 copy-start.2
  80.9 0.0 copy-start.3
  80.9 0.2 pad_maximum_fusion.far_nodes_ref
  81.1 0.0 all-to-all-done.1
  81.1 1.0 copy-done.2
  82.1 36.4 %far.1 = f32[64,64,128]{2,1,0:T(8,128)S(1)} custom-call(s32[64,96]{1,0:T(8,128)S(1)} %copy-done.3, bf16[64,16,64]{2,1,0:T(8,128)(2,1)S(1)} %concatenate.51.nodes_ref, bf16[256,2,16,128]{3,2,1,0:T(8,128)(2,1)S(1)} %pad_maximum_fusion.far_nodes_ref, bf16[256,32,128]{2,1,0:T(8,128)(2,1)} %bitcast.9.table_ref, bf16[64,64,128]{2,1,0:T(8,128)(2,1)S(1)} %copy-done.2), custom_call_target="tpu_custom_call" | custom-call | flops 15099494400 | bytes 8388608 | tf_op jit(solution)/shard_map/far/pallas_call | solution.py:214
  118.5 0.0 collective-permute-done.2
  118.5 0.0 collective-permute-done.3
  118.5 3.7 %add_add_fusion = f32[64,64,128]{2,1,0:T(8,128)} fusion(f32[64,64,128]{2,1,0:T(8,128)S(1)} %far.1, bf16[64,64,128]{2,1,0:T(8,128)(2,1)} %collective-permute-done.3, f32[64,64,128]{2,1,0:T(8,128)S(1)} %copy-done.4, bf16[64,64,128]{2,1,0:T(8,128)(2,1)} %collective-permute-done.2), kind=kLoop, calls=%fused_computation.2 | loop fusion | flops 2621440 | bytes 8388608 | tf_op jit(solution)/shard_map/add | solution.py:261
  (25 shorter events, 0.3 us)
Async XLA Ops:
  0.0 18.1 %copy-start.5 = (bf16[64,3,128]{2,0,1:T(8,128)(2,1)S(1)}, bf16[64,3,128]{2,0,1:T(8,128)(2,1)}, u32[]{:S(2)}) copy-start(bf16[64,3,128]{2,0,1:T(8,128)(2,1)} %param.11) | copy-start | bytes 147460
  0.0 18.2 %copy-start.6 = (s32[64,27]{0,1:T(8,128)S(1)}, s32[64,27]{0,1:T(8,128)}, u32[]{:S(2)}) copy-start(s32[64,27]{0,1:T(8,128)} %param.13) | copy-start | bytes 20740
  0.0 18.3 %copy-start.1 = (bf16[64,64,128]{2,1,0:T(8,128)(2,1)S(1)}, bf16[64,64,128]{2,1,0:T(8,128)(2,1)}, u32[]{:S(2)}) copy-start(bf16[64,64,128]{2,1,0:T(8,128)(2,1)} %density_ref.3) | copy-start | bytes 3145732
  0.0 18.3 %copy-start = (bf16[64,64,128]{2,1,0:T(8,128)(2,1)S(1)}, bf16[64,64,128]{2,1,0:T(8,128)(2,1)}, u32[]{:S(2)}) copy-start(bf16[64,64,128]{2,1,0:T(8,128)(2,1)} %basis_ref.2) | copy-start | bytes 3145732
  1.0 30.4 %collective-permute-start = (bf16[64,3,128]{2,1,0:T(4,128)(2,1)S(1)}, bf16[64,3,128]{2,1,0:T(4,128)(2,1)S(1)}, u32[]{:S(2)}, u32[]{:S(2)}) collective-permute-start(bf16[64,3,128]{2,1,0:T(4,128)(2,1)S(1)} %get-tuple-element.19), channel_id=1, source_target_pairs={{1,0},{2,1},{3,2},{5,4},{6,5},{7,6},{9,8},{10,9},{11,10},{13,12},{... | collective-permute-start | bytes 147464 | tf_op jit(solution)/shard_map/ppermute | solution.py:22
  2.3 29.2 %collective-permute-start.1 = (bf16[64,3,128]{2,1,0:T(4,128)(2,1)S(1)}, bf16[64,3,128]{2,1,0:T(4,128)(2,1)S(1)}, u32[]{:S(2)}, u32[]{:S(2)}) collective-permute-start(bf16[64,3,128]{2,1,0:T(4,128)(2,1)S(1)} %get-tuple-element.19), channel_id=1, source_target_pairs={{4,0},{8,4},{12,8},{16,12},{20,16},{24,20},{28,24},{5,1},{9,5},{13... | collective-permute-start | bytes 147464 | tf_op jit(solution)/shard_map/ppermute | solution.py:22
  7.3 17.3 %all-to-all-start = ((bf16[32,8,192]{2,1,0:T(8,128)(2,1)}), bf16[32,8,192]{2,1,0:T(8,128)(2,1)S(1)}, u32[]{:S(2)}, u32[]{:S(2)}) async-start(bf16[32,8,192]{2,1,0:T(8,128)(2,1)} %bitcast.3), calls=%async_computation | async-start | bytes 262144 | tf_op jit(solution)/shard_map/all_to_all | solution.py:246
  24.6 56.5 %all-to-all-start.1 = ((bf16[32,256,128]{2,1,0:T(8,128)(2,1)}), bf16[32,256,128]{2,1,0:T(8,128)(2,1)}, u32[]{:S(2)}, u32[]{:S(2)}) async-start(bf16[32,256,128]{2,1,0:T(8,128)(2,1)} %bitcast.8), calls=%async_computation.1 | async-start | bytes 4194304 | tf_op jit(solution)/shard_map/all_to_all | solution.py:247
  66.4 52.0 %collective-permute-start.2 = (bf16[64,64,128]{2,1,0:T(8,128)(2,1)}, bf16[64,64,128]{2,1,0:T(8,128)(2,1)}, u32[]{:S(2)}, u32[]{:S(2)}) collective-permute-start(bf16[64,64,128]{2,1,0:T(8,128)(2,1)} %get-tuple-element.9), channel_id=1, source_target_pairs={{0,1},{1,2},{2,3},{4,5},{5,6},{6,7},{8,9},{9,10},{10,11},{12,13},{... | collective-permute-start | bytes 3145736 | tf_op jit(solution)/shard_map/ppermute | solution.py:22
  69.5 48.9 %collective-permute-start.3 = (bf16[64,64,128]{2,1,0:T(8,128)(2,1)}, bf16[64,64,128]{2,1,0:T(8,128)(2,1)}, u32[]{:S(2)}, u32[]{:S(2)}) collective-permute-start(bf16[64,64,128]{2,1,0:T(8,128)(2,1)} %get-tuple-element.10), channel_id=1, source_target_pairs={{0,4},{4,8},{8,12},{12,16},{16,20},{20,24},{24,28},{1,5},{5,9},{9,... | collective-permute-start | bytes 3145736 | tf_op jit(solution)/shard_map/ppermute | solution.py:22
  80.9 1.2 %copy-start.2 = (bf16[64,64,128]{2,1,0:T(8,128)(2,1)S(1)}, bf16[64,64,128]{2,1,0:T(8,128)(2,1)}, u32[]{:S(2)}) copy-start(bf16[64,64,128]{2,1,0:T(8,128)(2,1)} %basis_ref.3) | copy-start | bytes 3145732
  80.9 1.2 copy-start.3
  82.1 36.4 %copy-start.4 = (f32[64,64,128]{2,1,0:T(8,128)S(1)}, f32[64,64,128]{2,1,0:T(8,128)}, u32[]{:S(2)}) copy-start(f32[64,64,128]{2,1,0:T(8,128)} %get-tuple-element.8) | copy-start | bytes 6291460

commit v3 on v2

--- a/solution.py
+++ b/solution.py
@@ -242,11 +242,14 @@
     wide_points = passed_along(points, "wide", -1)
     outgoing = outgoing_blocks(send, basis_in, density)
     outgoing = outgoing.reshape(devices, capacity * outgoing.shape[1], outgoing.shape[2])
-    out_nodes = nodes.reshape(leaves, -1)[send].reshape(devices, capacity, 3 * rank_size)
-    table_nodes = lax.all_to_all(out_nodes, axes, split_axis=0, concat_axis=0, tiled=True)
-    table = lax.all_to_all(outgoing, axes, split_axis=0, concat_axis=0, tiled=True)
-    table = table.reshape(devices * capacity, rank_size // 2, 2 * fields)
-    far_nodes = as_targets(table_nodes.reshape(devices * capacity, 3, rank_size))
+    block_rows = outgoing.shape[1]
+    padded = jnp.pad(nodes, ((0, 0), (0, 1), (0, 0))).reshape(leaves, -1)[send]
+    out_nodes = padded.reshape(devices, -1, outgoing.shape[2])
+    outgoing = jnp.concatenate([outgoing, out_nodes], axis=1)
+    arrived = lax.all_to_all(outgoing, axes, split_axis=0, concat_axis=0, tiled=True)
+    table = arrived[:, :block_rows].reshape(devices * capacity, rank_size // 2, 2 * fields)
+    table_nodes = arrived[:, block_rows:].reshape(devices * capacity, 4, rank_size)[:, :3]
+    far_nodes = as_targets(table_nodes)
     far_nodes = halves_repeated(far_nodes)
 
     my_device = lax.axis_index("wide") * deep_count + lax.axis_index("deep")

time: 123 us -> 162 us (1.32)
  the two profiles are of different devices: /device:TPU:0 before, /device:TPU:9 now
where the time goes in v3:
time: 162 us
  Pallas kernels  70.8 us (44%)
  starting transfers between devices  44.9 us (28%)
  waiting for transfers between devices  18.4 us (11%)
  local copies, waits for them, and re-layouts  17.3 us (11%)
  other arithmetic  9.91 us (6%)
    ppermute x4, starting transfers between devices, passed_along(): return lax.ppermute(x, axis, pairs)  38.5 us
    pallas_call x1, Pallas kernels, far_sums(): pl.pallas_call(far_kernel, out_shape=jax.ShapeDtypeStruct((leaves, fields...  36.3 us
    pallas_call x1, Pallas kernels, near_sums(): pl.pallas_call(near_kernel, out_shape=[jax.ShapeDtypeStruct(density.shape...  29.7 us
    ppermute x4, waiting for transfers between devices, passed_along(): return lax.ppermute(x, axis, pairs)  18.4 us
    concatenate x6, local copies, waits for them, and re-layouts, as_targets(): return jnp.concatenate(rows, axis=1).astype(jnp.bfloat16)  7.16 us
    all_to_all x1, starting transfers between devices, shards(): lax.all_to_all(outgoing, axes, split_axis=0, concat_axis=0, tiled=True)  6.41 us
    pallas_call x1, Pallas kernels, outgoing_blocks(): pl.pallas_call(outgoing_kernel, out_shape=jax.ShapeDtypeStruct((send.shap...  4.8 us
    add x1, other arithmetic, shards(): far_field + (own + from_deep.astype(jnp.float32) + from_wide.astype(jnp.f...  3.68 us
  transfers between devices with their start and end apart: 5, of which 2 were waited for; matrix products, arithmetic and copies ran while one was open for 11% of the time, Pallas kernels for 41%

profile of v3, /device:TPU:9, one launch (start us, length us, event | category | flops | bytes accessed | tf_op | source)
XLA Modules:
  0.0 161.7 jit_solution(16432013888727775925)
XLA Ops:
  0.0 0.8 copy.34
  0.9 0.1 reshape.172.send_ref
  0.9 0.1 reshape.175
  1.1 0.8 copy.46
  2.0 0.1 reshape.174
  2.1 1.2 gather_fusion
  3.3 0.0 copy-start.1
  3.3 1.2 copy-done.1
  4.5 4.8 %outgoing.1 = bf16[256,32,128]{2,1,0:T(8,128)(2,1)S(1)} custom-call(s32[256]{0:T(256)S(1)} %reshape.172.send_ref, bf16[64,64,128]{2,1,0:T(8,128)(2,1)S(1)} %copy-done, bf16[64,64,128]{2,1,0:T(8,128)(2,1)S(1)} %copy-done.1), custom_call_target="tpu_custom_call" | custom-call | tf_op jit(solution)/shard_map/outgoing/pallas_call | solution.py:91
  9.3 1.5 pad_maximum_fusion
  10.8 6.4 %all-to-all-start = ((bf16[32,272,128]{2,1,0:T(8,128)(2,1)}), bf16[32,272,128]{2,1,0:T(8,128)(2,1)}, u32[]{:S(2)}, u32[]{:S(2)}) async-start(bf16[32,272,128]{2,1,0:T(8,128)(2,1)} %pad_maximum_fusion), calls=%async_computation | async-start | bytes 4456448 | tf_op jit(solution)/shard_map/all_to_all | solution.py:249
  17.3 0.1 fusion.10
  17.3 2.3 %collective-permute-start = (bf16[64,3,128]{2,1,0:T(4,128)(2,1)S(1)}, bf16[64,3,128]{2,1,0:T(4,128)(2,1)S(1)}, u32[]{:S(2)}, u32[]{:S(2)}) collective-permute-start(bf16[64,3,128]{2,1,0:T(4,128)(2,1)S(1)} %get-tuple-element.19), channel_id=1, source_target_pairs={{1,0},{2,1},{3,2},{5,4},{6,5},{7,6},{9,8},{10,9},{11,10},{13,12},{... | collective-permute-start | bytes 147464 | tf_op jit(solution)/shard_map/ppermute | solution.py:22
  19.6 3.1 %collective-permute-start.1 = (bf16[64,3,128]{2,1,0:T(4,128)(2,1)S(1)}, bf16[64,3,128]{2,1,0:T(4,128)(2,1)S(1)}, u32[]{:S(2)}, u32[]{:S(2)}) collective-permute-start(bf16[64,3,128]{2,1,0:T(4,128)(2,1)S(1)} %get-tuple-element.19), channel_id=1, source_target_pairs={{4,0},{8,4},{12,8},{16,12},{20,16},{24,20},{28,24},{5,1},{9,5},{13... | collective-permute-start | bytes 147464 | tf_op jit(solution)/shard_map/ppermute | solution.py:22
  22.8 0.1 copy.38
  22.9 0.1 fusion.4
  23.0 0.1 fusion.5
  23.1 0.1 fusion.2
  23.2 0.1 fusion.1
  23.4 0.3 concatenate.54.nodes_ref
  23.7 0.0 copy-start.2
  23.7 0.3 concatenate.63.sources_ref
  24.0 7.4 %collective-permute-done = bf16[64,3,128]{2,1,0:T(4,128)(2,1)S(1)} collective-permute-done((bf16[64,3,128]{2,1,0:T(4,128)(2,1)S(1)}, bf16[64,3,128]{2,1,0:T(4,128)(2,1)S(1)}, u32[]{:S(2)}, u32[]{:S(2)}) %collective-permute-start) | collective-permute-done | bytes 49184 | tf_op jit(solution)/shard_map/ppermute | solution.py:22
  31.4 11.0 %collective-permute-done.1 = bf16[64,3,128]{2,1,0:T(4,128)(2,1)S(1)} collective-permute-done((bf16[64,3,128]{2,1,0:T(4,128)(2,1)S(1)}, bf16[64,3,128]{2,1,0:T(4,128)(2,1)S(1)}, u32[]{:S(2)}, u32[]{:S(2)}) %collective-permute-start.1) | collective-permute-done | bytes 49184 | tf_op jit(solution)/shard_map/ppermute | solution.py:22
  42.4 0.3 multiply_reduce_fusion.1
  42.7 0.2 fusion.3
  42.9 0.1 concatenate.66
  43.0 0.1 concatenate.65
  43.0 2.4 %concatenate.67.targets_ref = bf16[192,16,128]{2,1,0:T(8,128)(2,1)S(1)} concatenate(bf16[192,3,128]{2,1,0:T(4,128)(2,1)S(1)} %constant_dynamic-update-slice_fusion, bf16[192,1,128]{2,1,0:T(2,128)(2,1)S(1)} %get-tuple-element.18, bf16[192,1,128]{2,1,0:T(2,128)(2,1)S(1)} %get-tuple-element.17, bf16[192,1,128]{2,1,0:T(2,128)(2,1)S(1)} %get-tuple-element.16, ...), dimensions={1} | concatenate | bytes 1572864 | tf_op jit(solution)/shard_map/concatenate | solution.py:45
  45.5 29.7 %near.1 = (f32[64,64,128]{2,1,0:T(8,128)}, bf16[64,64,128]{2,1,0:T(8,128)(2,1)}, bf16[64,64,128]{2,1,0:T(8,128)(2,1)S(1)}) custom-call(s32[64,27]{1,0:T(8,128)S(1)} %fusion.7.codes_ref, bf16[64,16,128]{2,1,0:T(8,128)(2,1)S(1)} %concatenate.63.sources_ref, bf16[192,16,128]{2,1,0:T(8,128)(2,1)S(1)} %concatenate.67.targets_ref, bf16[64,64,128]{2,1,0:T(8,128)(2,1)S(1)} %copy-done.2), custom_call_target="tpu_custom_call" | custom-call | flops 16986931200 | bytes 16777216 | tf_op jit(solution)/shard_map/near/pallas_call | solution.py:141
  75.2 4.7 %collective-permute-start.2 = (bf16[64,64,128]{2,1,0:T(8,128)(2,1)}, bf16[64,64,128]{2,1,0:T(8,128)(2,1)}, u32[]{:S(2)}, u32[]{:S(2)}) collective-permute-start(bf16[64,64,128]{2,1,0:T(8,128)(2,1)} %get-tuple-element.9), channel_id=1, source_target_pairs={{0,1},{1,2},{2,3},{4,5},{5,6},{6,7},{8,9},{9,10},{10,11},{12,13},{... | collective-permute-start | bytes 3145736 | tf_op jit(solution)/shard_map/ppermute | solution.py:22
  79.8 28.5 %collective-permute-start.3 = (bf16[64,64,128]{2,1,0:T(8,128)(2,1)S(1)}, bf16[64,64,128]{2,1,0:T(8,128)(2,1)}, u32[]{:S(2)}, u32[]{:S(2)}) collective-permute-start(bf16[64,64,128]{2,1,0:T(8,128)(2,1)S(1)} %get-tuple-element.10), channel_id=1, source_target_pairs={{0,4},{4,8},{8,12},{12,16},{16,20},{20,24},{24,28},{1,5},{5,9},{9,... | collective-permute-start | bytes 3145736 | tf_op jit(solution)/shard_map/ppermute | solution.py:22
  108.3 0.9 slice.22
  109.3 0.1 reshape.177
  109.4 0.4 multiply_reduce_fusion
  109.8 1.1 fusion
  110.9 0.1 concatenate.57
  111.0 0.1 concatenate.56
  111.1 4.5 %concatenate.58 = bf16[256,16,64]{2,1,0:T(8,128)(2,1)S(1)} concatenate(bf16[256,3,64]{2,1,0:T(4,128)(2,1)S(1)} %bitcast.15, bf16[256,1,64]{2,1,0:T(2,128)(2,1)} %get-tuple-element.15, bf16[256,1,64]{2,1,0:T(2,128)(2,1)} %get-tuple-element.14, bf16[256,1,64]{2,1,0:T(2,128)(2,1)} %get-tuple-element.13, bf16[256,3,64]{2,1,0:T(4,128)(2,1)S(1)} %concatenate.56, ...), dimensions={1} | concatenate | bytes 1048576 | tf_op jit(solution)/shard_map/concatenate | solution.py:45
  115.6 0.5 fusion.9
  116.1 2.1 %maximum_bitcast_fusion = (bf16[256,1,16,128]{3,2,1,0:T(8,128)(2,1)S(1)}, bf16[256,1,16,128]{3,2,1,0:T(8,128)(2,1)S(1)}) fusion(bf16[256,16,32]{2,1,0:T(8,128)(2,1)S(1)} %get-tuple-element.11, bf16[256,16,32]{2,1,0:T(8,128)(2,1)S(1)} %get-tuple-element.12), kind=kLoop, calls=%fused_computation.4 | loop fusion | flops 8388608 | bytes 2621440 | tf_op jit(solution)/shard_map/stack | solution.py:230
  118.2 0.2 pad_maximum_fusion.1.far_nodes_ref
  118.4 0.0 copy-start.3
  118.4 0.0 copy-start.4
  118.5 3.2 %slice.26 = bf16[32,256,128]{2,1,0:T(8,128)(2,1)} slice(bf16[32,272,128]{2,1,0:T(8,128)(2,1)} %all-to-all-done), slice={[0:32], [0:256], [0:128]} | slice | bytes 4194304 | tf_op jit(solution)/shard_map/slice | solution.py:250
  121.7 36.3 %far.1 = f32[64,64,128]{2,1,0:T(8,128)S(1)} custom-call(s32[64,96]{1,0:T(8,128)S(1)} %copy-done.4, bf16[64,16,64]{2,1,0:T(8,128)(2,1)S(1)} %concatenate.54.nodes_ref, bf16[256,2,16,128]{3,2,1,0:T(8,128)(2,1)S(1)} %pad_maximum_fusion.1.far_nodes_ref, bf16[256,32,128]{2,1,0:T(8,128)(2,1)} %bitcast.16, bf16[64,64,128]{2,1,0:T(8,128)(2,1)S(1)} %copy-done.3), custom_call_target="tpu_custom_call" | custom-call | flops 15099494400 | bytes 8388608 | tf_op jit(solution)/shard_map/far/pallas_call | solution.py:214
  158.0 0.0 collective-permute-done.3
  158.1 3.7 %add_add_fusion = f32[64,64,128]{2,1,0:T(8,128)} fusion(f32[64,64,128]{2,1,0:T(8,128)S(1)} %far.1, bf16[64,64,128]{2,1,0:T(8,128)(2,1)} %collective-permute-done.3, f32[64,64,128]{2,1,0:T(8,128)S(1)} %copy-done.5, bf16[64,64,128]{2,1,0:T(8,128)(2,1)} %collective-permute-done.2), kind=kLoop, calls=%fused_computation.3 | loop fusion | flops 2621440 | bytes 8388608 | tf_op jit(solution)/shard_map/add | solution.py:264
  (32 shorter events, 0.4 us)
Async XLA Ops:
  0.0 3.3 %copy-start = (bf16[64,64,128]{2,1,0:T(8,128)(2,1)S(1)}, bf16[64,64,128]{2,1,0:T(8,128)(2,1)}, u32[]{:S(2)}) copy-start(bf16[64,64,128]{2,1,0:T(8,128)(2,1)} %basis_ref.2) | copy-start | bytes 3145732
  3.3 1.2 copy-start.1
  10.8 6.4 %copy-start.7 = (bf16[64,3,128]{2,0,1:T(8,128)(2,1)S(1)}, bf16[64,3,128]{2,0,1:T(8,128)(2,1)}, u32[]{:S(2)}) copy-start(bf16[64,3,128]{2,0,1:T(8,128)(2,1)} %param.11) | copy-start | bytes 147460
  10.8 11.9 %copy-start.6 = (bf16[64,3,64]{2,0,1:T(8,128)(2,1)S(1)}, bf16[64,3,64]{2,0,1:T(8,128)(2,1)}, u32[]{:S(2)}) copy-start(bf16[64,3,64]{2,0,1:T(8,128)(2,1)} %param.12) | copy-start | bytes 73732
  10.8 11.9 %copy-start.8 = (s32[64,27]{0,1:T(8,128)S(1)}, s32[64,27]{0,1:T(8,128)}, u32[]{:S(2)}) copy-start(s32[64,27]{0,1:T(8,128)} %param.13) | copy-start | bytes 20740
  10.8 97.5 %all-to-all-start = ((bf16[32,272,128]{2,1,0:T(8,128)(2,1)}), bf16[32,272,128]{2,1,0:T(8,128)(2,1)}, u32[]{:S(2)}, u32[]{:S(2)}) async-start(bf16[32,272,128]{2,1,0:T(8,128)(2,1)} %pad_maximum_fusion), calls=%async_computation | async-start | bytes 4456448 | tf_op jit(solution)/shard_map/all_to_all | solution.py:249
  17.3 14.1 %collective-permute-start = (bf16[64,3,128]{2,1,0:T(4,128)(2,1)S(1)}, bf16[64,3,128]{2,1,0:T(4,128)(2,1)S(1)}, u32[]{:S(2)}, u32[]{:S(2)}) collective-permute-start(bf16[64,3,128]{2,1,0:T(4,128)(2,1)S(1)} %get-tuple-element.19), channel_id=1, source_target_pairs={{1,0},{2,1},{3,2},{5,4},{6,5},{7,6},{9,8},{10,9},{11,10},{13,12},{... | collective-permute-start | bytes 147464 | tf_op jit(solution)/shard_map/ppermute | solution.py:22
  19.6 22.8 %collective-permute-start.1 = (bf16[64,3,128]{2,1,0:T(4,128)(2,1)S(1)}, bf16[64,3,128]{2,1,0:T(4,128)(2,1)S(1)}, u32[]{:S(2)}, u32[]{:S(2)}) collective-permute-start(bf16[64,3,128]{2,1,0:T(4,128)(2,1)S(1)} %get-tuple-element.19), channel_id=1, source_target_pairs={{4,0},{8,4},{12,8},{16,12},{20,16},{24,20},{28,24},{5,1},{9,5},{13... | collective-permute-start | bytes 147464 | tf_op jit(solution)/shard_map/ppermute | solution.py:22
  23.7 21.8 %copy-start.2 = (bf16[64,64,128]{2,1,0:T(8,128)(2,1)S(1)}, bf16[64,64,128]{2,1,0:T(8,128)(2,1)}, u32[]{:S(2)}) copy-start(bf16[64,64,128]{2,1,0:T(8,128)(2,1)} %density_ref.3) | copy-start | bytes 3145732
  75.2 82.9 %collective-permute-start.2 = (bf16[64,64,128]{2,1,0:T(8,128)(2,1)}, bf16[64,64,128]{2,1,0:T(8,128)(2,1)}, u32[]{:S(2)}, u32[]{:S(2)}) collective-permute-start(bf16[64,64,128]{2,1,0:T(8,128)(2,1)} %get-tuple-element.9), channel_id=1, source_target_pairs={{0,1},{1,2},{2,3},{4,5},{5,6},{6,7},{8,9},{9,10},{10,11},{12,13},{... | collective-permute-start | bytes 3145736 | tf_op jit(solution)/shard_map/ppermute | solution.py:22
  79.8 78.2 %collective-permute-start.3 = (bf16[64,64,128]{2,1,0:T(8,128)(2,1)S(1)}, bf16[64,64,128]{2,1,0:T(8,128)(2,1)}, u32[]{:S(2)}, u32[]{:S(2)}) collective-permute-start(bf16[64,64,128]{2,1,0:T(8,128)(2,1)S(1)} %get-tuple-element.10), channel_id=1, source_target_pairs={{0,4},{4,8},{8,12},{12,16},{16,20},{20,24},{24,28},{1,5},{5,9},{9,... | collective-permute-start | bytes 3145736 | tf_op jit(solution)/shard_map/ppermute | solution.py:22
  118.4 3.3 %copy-start.3 = (bf16[64,64,128]{2,1,0:T(8,128)(2,1)S(1)}, bf16[64,64,128]{2,1,0:T(8,128)(2,1)}, u32[]{:S(2)}) copy-start(bf16[64,64,128]{2,1,0:T(8,128)(2,1)} %basis_ref.3) | copy-start | bytes 3145732
  118.4 3.2 %copy-start.4 = (s32[64,96]{1,0:T(8,128)S(1)}, s32[64,96]{1,0:T(8,128)}, u32[]{:S(2)}) copy-start(s32[64,96]{1,0:T(8,128)} %slots_ref.1) | copy-start | bytes 73732
  121.7 36.4 %copy-start.5 = (f32[64,64,128]{2,1,0:T(8,128)S(1)}, f32[64,64,128]{2,1,0:T(8,128)}, u32[]{:S(2)}) copy-start(f32[64,64,128]{2,1,0:T(8,128)} %get-tuple-element.8) | copy-start | bytes 6291460
